TPU v7x, 32 devices: a whole 2x2x4 slice. The times are simulated.
32 devices in a mesh: groups: 2 (over x), dp: 16 (over z, y, core).
Axes of the slice: x: 2, y: 2, z: 4, core: 2. Of those that a mesh axis runs over, the one named last changes fastest.
Arguments:
- train_grads: bfloat16 [32768, 1024], P(('groups', 'dp')), parts along dimension 0, as said below
- eval_grads: bfloat16 [2048, 1024], P(('groups', 'dp')), parts along dimension 0, may hold values from -6 to 6
- pair_eval: int32 [32, 4], P('groups'), parts along dimension 0, may hold values from 0 to 3, each once within a row
- pair_count: int32 [32], P('groups'), parts along dimension 0, may hold values from 1 to 4, as said below
Outputs:
- influence: float32 [4, 32768], P(None, ('groups', 'dp')), parts along dimension 1
There are 2 independent parts, one for each index of `groups`. A program takes and returns all parts, laid end to end along the dimension named above; each array names one. Nothing has to cross between parts.
Inputs may be any that keep to these rules, and one draw needn't show every extreme that they name: `train_grads`: entries are real-valued gradients of varying scale. `pair_count`: the largest count equals 4 in every draw.
All inputs are finite; a program needn't handle non-finite values.
Results may differ from a plain program's by a relative error of at most 0.0015.
Values may be sent and summed in bfloat16 or wider, within the bound.
No kernel may reach another device: no remote copies, remote signals or barrier semaphores. Data moves between devices by JAX's collectives and lax.ppermute only.
A program may use at most 64 MiB of HBM per device.

v0:
```python
import jax
import jax.numpy as jnp
from jax import lax
from jax.sharding import PartitionSpec as P

EB = 256


DAMPING = 0.1
EPSILON = 1e-06


def inverse_norms(rows):
    return lax.rsqrt(jnp.sum(jnp.square(rows.astype(jnp.float32)), axis=1) + EPSILON)


def block_tops(rows, scale, eval_block):
    score = lax.dot_general(
        rows, eval_block, (((1,), (1,)), ((), ())), preferred_element_type=jnp.float32
    )
    return jnp.max(score, axis=1) * scale


def per_device(train_grads, eval_grads, pair_eval, pair_count):
    width = train_grads.shape[1]
    tr_rows = train_grads.shape[0]
    local_gram = lax.dot_general(
        train_grads, train_grads, (((0,), (0,)), ((), ())), preferred_element_type=jnp.float32
    )
    summed = lax.psum(local_gram, "dp")
    trace = jnp.trace(summed)
    gram = summed * (width / trace) + DAMPING * jnp.eye(width, dtype=jnp.float32)
    factor = jnp.linalg.cholesky(gram)
    half = lax.linalg.triangular_solve(
        factor, eval_grads.astype(jnp.float32), left_side=False, lower=True, transpose_a=True
    )
    precond = lax.linalg.triangular_solve(factor, half, left_side=False, lower=True).astype(
        jnp.bfloat16
    )
    every_eval = lax.all_gather(precond, "dp", axis=0, tiled=True)
    num_blocks = every_eval.shape[0] // EB
    evals = every_eval.reshape(num_blocks, EB, width)
    scale = inverse_norms(train_grads)
    me = lax.axis_index("dp")
    order = pair_eval[me]
    count = pair_count[me]

    def one_pair(slot, result):
        target = order[slot]
        eval_block = lax.dynamic_index_in_dim(evals, target, 0, keepdims=False)
        tops = block_tops(train_grads, scale, eval_block)
        return lax.dynamic_update_slice(result, tops[None, :], (target, jnp.int32(0)))

    start = jnp.zeros((num_blocks, tr_rows), jnp.float32)
    return lax.fori_loop(jnp.int32(0), count, one_pair, start)


def solution(mesh):
    placed = (P(("groups", "dp"), None), P(("groups", "dp"), None), P("groups", None), P("groups"))
    return jax.shard_map(
        per_device, mesh=mesh, in_specs=placed, out_specs=P(None, ("groups", "dp")), check_vma=False
    )
```

profile of v0, /device:TPU:21, one launch (start us, length us, event | category | flops | bytes accessed | tf_op | source)
XLA Modules:
  0.0 550.1 jit_solution(10763115708969255769)
XLA Ops:
  6.5 6.6 %fusion.99 = f32[1024,1024]{0,1:T(8,128)} fusion(bf16[1024,1024]{1,0:T(8,128)(2,1)} %param.6), kind=kOutput, calls=%fused_computation.224 | convolution fusion | flops 2147483648 | bytes 6291456 | tf_op jit(solution)/shard_map/dot_general | solution.py:27
  14.1 110.4 %all-reduce.3.cloned.1.call-done = f32[1024,1024]{0,1:T(8,128)} async-done(((f32[1024,1024]{0,1:T(8,128)}), f32[1024,1024]{0,1:T(8,128)}) %all-reduce.3.cloned.1.call-update) | async-done | bytes 4194320 | tf_op jit(solution)/shard_map/psum | solution.py:30
  124.5 2.9 select_reduce_fusion
  128.1 5.0 select_add_fusion
  133.1 5.5 copy.6
  138.6 4.5 fusion.3
  145.0 11.7 %cholesky.222 = f32[128,128]{1,0:T(8,128)S(1)} custom-call(f32[128,128]{1,0:T(8,128)S(1)} %cholesky.577), custom_call_target="Cholesky" | custom-call | tf_op jit(solution)/shard_map/jit(cholesky)/cholesky | solution.py:33
  156.9 9.8 %custom-call.64 = f32[1,128,128]{1,2,0:T(8,128)S(1)} custom-call(f32[1,128,128]{2,1,0:T(8,128)S(1)} %get-tuple-element.93), custom_call_target="InvertDiagBlocksLowerTriangular" | custom-call | tf_op jit(solution)/shard_map/jit(cholesky)/cholesky | solution.py:33
  170.0 11.7 %cholesky.243 = f32[128,128]{1,0:T(8,128)S(1)} custom-call(f32[128,128]{1,0:T(8,128)S(1)} %cholesky.581), custom_call_target="Cholesky" | custom-call | tf_op jit(solution)/shard_map/jit(cholesky)/cholesky | solution.py:33
  182.0 9.8 %custom-call.65 = f32[1,128,128]{1,2,0:T(8,128)S(1)} custom-call(f32[1,128,128]{2,1,0:T(8,128)S(1)} %get-tuple-element.91), custom_call_target="InvertDiagBlocksLowerTriangular" | custom-call | tf_op jit(solution)/shard_map/jit(cholesky)/cholesky | solution.py:33
  194.9 2.4 convolution_subtract_fusion.1
  197.4 11.7 %cholesky.466 = f32[128,128]{1,0:T(8,128)S(1)} custom-call(f32[128,128]{1,0:T(8,128)S(1)} %cholesky.586), custom_call_target="Cholesky" | custom-call | tf_op jit(solution)/shard_map/jit(cholesky)/cholesky | solution.py:33
  209.8 9.8 %custom-call.66 = f32[1,128,128]{1,2,0:T(8,128)S(1)} custom-call(f32[1,128,128]{2,1,0:T(8,128)S(1)} %get-tuple-element.89), custom_call_target="InvertDiagBlocksLowerTriangular" | custom-call | tf_op jit(solution)/shard_map/jit(cholesky)/cholesky | solution.py:33
  220.9 3.6 convolution_subtract_fusion.2
  224.5 11.7 %cholesky.485 = f32[128,128]{1,0:T(8,128)S(1)} custom-call(f32[128,128]{1,0:T(8,128)S(1)} %cholesky.591), custom_call_target="Cholesky" | custom-call | tf_op jit(solution)/shard_map/jit(cholesky)/cholesky | solution.py:33
  237.0 9.8 %custom-call.67 = f32[1,128,128]{1,2,0:T(8,128)S(1)} custom-call(f32[1,128,128]{2,1,0:T(8,128)S(1)} %get-tuple-element.87), custom_call_target="InvertDiagBlocksLowerTriangular" | custom-call | tf_op jit(solution)/shard_map/jit(cholesky)/cholesky | solution.py:33
  247.9 3.2 convolution_subtract_fusion.3
  251.1 11.9 %cholesky.504 = f32[128,128]{1,0:T(8,128)S(1)} custom-call(f32[128,128]{1,0:T(8,128)S(1)} %cholesky.596), custom_call_target="Cholesky" | custom-call | tf_op jit(solution)/shard_map/jit(cholesky)/cholesky | solution.py:33
  263.7 9.8 %custom-call.68 = f32[1,128,128]{1,2,0:T(8,128)S(1)} custom-call(f32[1,128,128]{2,1,0:T(8,128)S(1)} %get-tuple-element.85), custom_call_target="InvertDiagBlocksLowerTriangular" | custom-call | tf_op jit(solution)/shard_map/jit(cholesky)/cholesky | solution.py:33
  274.7 3.1 convolution_subtract_fusion.4
  277.8 11.7 %cholesky.524 = f32[128,128]{1,0:T(8,128)S(1)} custom-call(f32[128,128]{1,0:T(8,128)S(1)} %cholesky.601), custom_call_target="Cholesky" | custom-call | tf_op jit(solution)/shard_map/jit(cholesky)/cholesky | solution.py:33
  290.3 9.8 %custom-call.69 = f32[1,128,128]{1,2,0:T(8,128)S(1)} custom-call(f32[1,128,128]{2,1,0:T(8,128)S(1)} %get-tuple-element.83), custom_call_target="InvertDiagBlocksLowerTriangular" | custom-call | tf_op jit(solution)/shard_map/jit(cholesky)/cholesky | solution.py:33
  301.1 2.9 convolution_subtract_fusion.5
  304.0 11.7 %cholesky.544 = f32[128,128]{1,0:T(8,128)S(1)} custom-call(f32[128,128]{1,0:T(8,128)S(1)} %cholesky.606), custom_call_target="Cholesky" | custom-call | tf_op jit(solution)/shard_map/jit(cholesky)/cholesky | solution.py:33
  316.5 9.8 %custom-call.70 = f32[1,128,128]{1,2,0:T(8,128)S(1)} custom-call(f32[1,128,128]{2,1,0:T(8,128)S(1)} %get-tuple-element.81), custom_call_target="InvertDiagBlocksLowerTriangular" | custom-call | tf_op jit(solution)/shard_map/jit(cholesky)/cholesky | solution.py:33
  329.3 11.7 %cholesky.562 = f32[128,128]{1,0:T(8,128)S(1)} custom-call(f32[128,128]{1,0:T(8,128)S(1)} %convolution_subtract_fusion.6), custom_call_target="Cholesky" | custom-call | tf_op jit(solution)/shard_map/jit(cholesky)/cholesky | solution.py:33
  351.5 4.8 select_select_fusion
  356.3 23.7 %while.12 = (s32[]{:T(128)}, f32[1024,1024]{0,1:T(8,128)}, s32[8,2]{0,1:T(2,128)S(1)}, f32[8,128,128]{2,1,0:T(8,128)S(1)}, s32[]{:T(128)}) while((s32[]{:T(128)}, f32[1024,1024]{0,1:T(8,128)}, s32[8,2]{0,1:T(2,128)S(1)}, f32[8,128,128]{2,1,0:T(8,128)S(1)}, s32[]{:T(128)}) %tuple.63), condition=%wide.while_cond, body=%wide.while_body.sunk | while | flops 2 | bytes 393329 | solution.py:34
  356.9 2.2 dynamic-slice.7
  380.1 78.8 %custom-call.71 = f32[8,128,128]{1,2,0:T(8,128)S(1)} custom-call(f32[8,128,128]{2,1,0:T(8,128)S(1)} %get-tuple-element.51), custom_call_target="InvertDiagBlocksLowerTriangular" | custom-call | tf_op jit(solution)/shard_map/triangular_solve | solution.py:34
  483.2 38.1 %all-gather.2.cloned.1.call-done = bf16[1024,1024]{1,0:T(8,128)(2,1)} async-done(((bf16[64,1024]{1,0:T(8,128)(2,1)}), bf16[1024,1024]{1,0:T(8,128)(2,1)}) %all-gather.2.cloned.1.call-update) | async-done | bytes 2097168 | tf_op jit(solution)/shard_map/all_gather | solution.py:40
  521.3 20.9 %while.11 = (s32[]{:T(128)}, f32[4,1024]{1,0:T(4,128)S(1)}, s32[]{:T(128)}, s32[4]{0:T(128)S(1)}, bf16[4,256,1024]{2,1,0:T(8,128)(2,1)}, /*index=5*/bf16[1024,10...) while((s32[]{:T(128)}, f32[4,1024]{1,0:T(4,128)S(1)}, s32[]{:T(128)}, ...), condition=%wide.region_21.22_spmd, body=%wide.region_19.21_spmd.sunk | while | flops 537133056 | bytes 2646213 | solution.py:55
  (185 shorter events, 82.2 us)
Async XLA Ops:
  6.5 476.0 %copy-start = (s32[16,4]{0,1:T(4,128)S(1)}, s32[16,4]{0,1:T(4,128)}, u32[]{:S(2)}) copy-start(s32[16,4]{0,1:T(4,128)} %param.8) | copy-start | bytes 772
  6.5 118.0 %all-reduce.3.cloned.1.call-start = ((), (), s32[]{:S(2)}) async-start(), calls=%async_computation | async-start | bytes 8388608 | tf_op jit(solution)/shard_map/psum | solution.py:30
  13.1 0.9 copy-start.4
  13.2 508.2 %all-gather.2.cloned.1.call-start = ((), (), s32[]{:S(2)}) async-start(), calls=%async_computation.1 | async-start | bytes 2228224 | tf_op jit(solution)/shard_map/all_gather | solution.py:40
  143.1 1.9 copy-start.2
  193.0 2.0 copy-start.1
  464.3 17.6 %copy-start.7 = (s32[16]{0:T(128)S(1)}, s32[16]{0:T(128)}, u32[]{:S(2)}) copy-start(s32[16]{0:T(128)} %param.9) | copy-start | bytes 196
  464.5 18.3 %copy-start.3 = (bf16[1024,1024]{1,0:T(8,128)(2,1)S(1)}, bf16[1024,1024]{1,0:T(8,128)(2,1)}, u32[]{:S(2)}) copy-start(bf16[1024,1024]{1,0:T(8,128)(2,1)} %param.6) | copy-start | bytes 6291460
  481.2 0.7 copy-start.5
  542.2 0.6 copy-start.6
Sparse Core Ops, SparseCore 0:
  13.3 111.1 all-reduce.2
  482.0 39.2 all-gather.1
where the time goes:
time: 558 us; the launch traced here: 550 us
  other arithmetic  264 us (47%)
  waiting for transfers between devices  149 us (27%)
  matrix products  61.8 us (11%)
  local copies, waits for them, and re-layouts  44.1 us (8%)
  between operations  20.2 us (4%)
  loops' own time  11.2 us (2%)
    another operation x30, other arithmetic, per_device(): factor = jnp.linalg.cholesky(gram)  167 us
    psum x1, waiting for transfers between devices, per_device(): summed = lax.psum(local_gram, 'dp')  110 us
    another operation x3, other arithmetic, per_device(): lax.linalg.triangular_solve(factor, eval_grads.astype(jnp.float32), left_...  83.7 us
    all_gather x1, waiting for transfers between devices, per_device(): every_eval = lax.all_gather(precond, 'dp', axis=0, tiled=True)  38.1 us
    another operation x14, matrix products, per_device(): factor = jnp.linalg.cholesky(gram)  26.2 us
    another operation x40, local copies, waits for them, and re-layouts  23.5 us
    another operation x15, matrix products, per_device(): lax.linalg.triangular_solve(factor, half, left_side=False, lower=True)  11.5 us
  transfers between devices with their start and end apart: 2, of which 2 were waited for; matrix products, arithmetic and copies ran while one was open for 0% of the time, Pallas kernels for 0%

commit v1 on v0

v1 whole, which is shorter than its diff:
```python
import functools

import jax
import jax.numpy as jnp
from jax import lax
from jax.experimental import pallas as pl
from jax.experimental.pallas import tpu as pltpu
from jax.sharding import PartitionSpec as P

EB = 256
DAMPING = 0.1
EPSILON = 1e-06
B = 128
F32, BF16 = jnp.float32, jnp.bfloat16
NT = (((1,), (1,)), ((), ()))
NN = (((1,), (0,)), ((), ()))
TN = (((0,), (0,)), ((), ()))
VMEM_BYTES = 56 * 1024 * 1024


def dot(a, b, dims):
    return lax.dot_general(a, b, dims, preferred_element_type=F32)


def slab_offset(j, nb):
    return B * (j * nb - j * (j - 1) // 2)


def split3(x):
    hi = x.astype(BF16)
    rest = x - hi.astype(F32)
    mid = rest.astype(BF16)
    lo = (rest - mid.astype(F32)).astype(BF16)
    return hi, mid, lo


def left_parts(x):
    h, m, l = split3(x)
    return jnp.concatenate([h, h, m, m, h, l], axis=1)


def right_parts(x, axis=1):
    h, m, l = split3(x)
    return jnp.concatenate([h, m, h, m, l, h], axis=axis)


def gram_kernel(me_ref, t_ref, out_ref, packed, *, nb, pieces):
    width = nb * B
    for J in range(nb // 2):
        c0 = 2 * B * J
        g = dot(t_ref[:, c0:], t_ref[:, c0 : c0 + 2 * B], TN)
        o0, o1 = slab_offset(2 * J, nb), slab_offset(2 * J + 1, nb)
        packed[o0 : o0 + width - c0, :] = g[:, :B]
        packed[o1 : o1 + width - c0 - B, :] = g[B:, B:]
    rows = packed.shape[0] // pieces
    me = me_ref[0]
    for r in range(pieces):
        to = pl.multiple_of((me ^ r) * rows, 8)
        out_ref[pl.ds(to, rows), :] = packed[r * rows : (r + 1) * rows, :]


def local_gram(me, t, pieces):
    nb = t.shape[1] // B
    total = slab_offset(nb, nb)
    return pl.pallas_call(
        functools.partial(gram_kernel, nb=nb, pieces=pieces),
        out_shape=jax.ShapeDtypeStruct((total, B), F32),
        in_specs=[
            pl.BlockSpec(memory_space=pltpu.SMEM),
            pl.BlockSpec(memory_space=pltpu.VMEM),
        ],
        out_specs=pl.BlockSpec(memory_space=pltpu.VMEM),
        scratch_shapes=[pltpu.VMEM((total, B), F32)],
        compiler_params=pltpu.CompilerParams(vmem_limit_bytes=VMEM_BYTES),
        cost_estimate=pl.CostEstimate(
            flops=t.shape[0] * t.shape[1] * t.shape[1],
            bytes_accessed=t.size * 2 + total * B * 4,
            transcendentals=0,
        ),
        name="local_gram",
    )(me, t)


def invert_block(M):
    M = list(M)
    full = (8, B)
    lane = lax.broadcasted_iota(jnp.int32, full, 1)
    sub = lax.broadcasted_iota(jnp.int32, full, 0)
    n = len(M)
    for b in range(n):
        k0 = 8 * b
        R = [jnp.broadcast_to(M[b][i : i + 1, :], full) for i in range(8)]
        S = [
            [jnp.broadcast_to(R[i][:, k0 + j : k0 + j + 1], full) for j in range(i + 1)]
            for i in range(8)
        ]
        inside = (lane >= k0) & (lane < k0 + 8)
        R = [
            jnp.where(inside, jnp.where(lane == k0 + i, 1.0, 0.0).astype(F32), R[i])
            for i in range(8)
        ]
        m = [[None] * 8 for _ in range(8)]
        rc = [None] * 8
        for j in range(8):
            rc[j] = 1.0 / S[j][j]
            for i in range(j + 1, 8):
                m[i][j] = S[i][j] * rc[j]
            for i in range(j + 1, 8):
                for k in range(j + 1, i + 1):
                    S[i][k] = S[i][k] - m[i][j] * S[k][j]
            for i in range(j + 1, 8):
                R[i] = R[i] - m[i][j] * R[j]
        for i in range(7, -1, -1):
            R[i] = R[i] * rc[i]
            for j in range(i + 1, 8):
                R[i] = R[i] - m[j][i] * R[j]
        for q in range(1, n + 1):
            t = (b + q) % n
            if t == b:
                x = R[0]
                for i in range(1, 8):
                    x = jnp.where(sub == i, R[i], x)
            else:
                c = [jnp.broadcast_to(M[t][:, k0 + k : k0 + k + 1], full) for k in range(8)]
                x = jnp.where(inside, 0.0, M[t])
                for k in range(8):
                    x = x - c[k] * R[k]
            M[t] = x
    return M


def inverse_kernel(me_ref, g_ref, hi_ref, lo_ref, packed, A, D, WL, CR, *, nb, pieces):
    width = nb * B
    rows = packed.shape[0] // pieces
    me = me_ref[0]
    for r in range(pieces):
        at = pl.multiple_of((me ^ r) * rows, 8)
        packed[r * rows : (r + 1) * rows, :] = g_ref[pl.ds(at, rows), :]
    eye = lax.broadcasted_iota(jnp.int32, (B, B), 0) == lax.broadcasted_iota(
        jnp.int32, (B, B), 1
    )
    diag = jnp.zeros((B, B), F32)
    for j in range(nb):
        o = slab_offset(j, nb)
        diag = diag + jnp.where(eye, packed[o : o + B, :], 0.0)
    trace = jnp.sum(jnp.sum(diag, axis=1, keepdims=True), axis=0, keepdims=True)
    scale = jnp.broadcast_to(width / trace, (1, B))
    damp = jnp.where(eye, DAMPING, 0.0).astype(F32)
    for j in range(nb):
        o = slab_offset(j, nb)
        A[j, B * j : B * j + B, :] = packed[o : o + B, :] * scale + damp
        if j + 1 < nb:
            A[j, B * j + B :, :] = packed[o + B : o + width - B * j, :] * scale
    D[...] = A[0, :B, :]
    WL[...] = jnp.zeros_like(WL)
    CR[...] = jnp.zeros_like(CR)
    MC = 256

    def update():
        for J in range(nb // 2):
            right = CR[2 * B * J : 2 * B * (J + 1), :]
            for r in range(0, width, MC):
                u = dot(WL[r : r + MC, :], right, NT)
                A[2 * J, r : r + MC, :] = A[2 * J, r : r + MC, :] - u[:, :B]
                A[2 * J + 1, r : r + MC, :] = A[2 * J + 1, r : r + MC, :] - u[:, B:]

    def step(k, carry):
        inv = jnp.concatenate(invert_block([D[8 * t : 8 * t + 8, :] for t in range(B // 8)]))
        update()
        own = pl.ds(pl.multiple_of(k * B, B), B)
        A[k, own, :] = jnp.zeros((B, B), F32)
        C = A[k]
        CR[...] = right_parts(C)
        W = dot(left_parts(C), right_parts(inv, axis=0), NN)
        A[k] = W
        WL[...] = left_parts(W)
        A[k, own, :] = -inv
        WL[own, :] = left_parts(-inv)
        for j in range(nb):
            @pl.when(j != k)
            def _():
                A[j, own, :] = jnp.zeros((B, B), F32)

        @pl.when(k + 1 < nb)
        def _():
            nxt = pl.ds(pl.multiple_of((k + 1) * B, B), B)
            D[...] = A[k + 1, nxt, :] - dot(WL[nxt, :], CR[nxt, :], NT)

        return carry

    lax.fori_loop(0, nb, step, 0)
    update()
    for j in range(nb):
        x = -A[j]
        hi = x.astype(BF16)
        hi_ref[:, B * j : B * j + B] = hi
        lo_ref[:, B * j : B * j + B] = (x - hi.astype(F32)).astype(BF16)


def gram_inverse(me, g, nb, pieces):
    width = nb * B
    out = jax.ShapeDtypeStruct((width, width), BF16)
    return pl.pallas_call(
        functools.partial(inverse_kernel, nb=nb, pieces=pieces),
        out_shape=(out, out),
        in_specs=[
            pl.BlockSpec(memory_space=pltpu.SMEM),
            pl.BlockSpec(memory_space=pltpu.VMEM),
        ],
        out_specs=(pl.BlockSpec(memory_space=pltpu.VMEM),) * 2,
        scratch_shapes=[
            pltpu.VMEM(g.shape, F32),
            pltpu.VMEM((nb, width, B), F32),
            pltpu.VMEM((B, B), F32),
            pltpu.VMEM((width, 6 * B), BF16),
            pltpu.VMEM((width, 6 * B), BF16),
        ],
        compiler_params=pltpu.CompilerParams(vmem_limit_bytes=VMEM_BYTES),
        cost_estimate=pl.CostEstimate(
            flops=12 * width**3, bytes_accessed=g.size * 4 + width * width * 4, transcendentals=0
        ),
        name="gram_inverse",
    )(me, g)


def score_kernel(flag_ref, e_ref, hi_ref, lo_ref, t_ref, scale_ref, out_ref):
    e = pl.program_id(0)

    @pl.when(flag_ref[e] > 0)
    def _():
        rows = e_ref[...]
        pre = (dot(rows, hi_ref[...], NN) + dot(rows, lo_ref[...], NN)).astype(BF16)
        score = dot(pre, t_ref[...], NT)
        out_ref[pl.ds(e, 1), :] = jnp.max(score, axis=0, keepdims=True) * scale_ref[...]

    @pl.when(flag_ref[e] <= 0)
    def _():
        out_ref[pl.ds(e, 1), :] = jnp.zeros((1, out_ref.shape[1]), F32)


def scores(flags, evals, hi, lo, t, scale):
    blocks = evals.shape[0] // EB
    width = t.shape[1]
    whole = lambda shape: pl.BlockSpec(shape, lambda e: (0, 0))
    return pl.pallas_call(
        score_kernel,
        grid=(blocks,),
        out_shape=jax.ShapeDtypeStruct((blocks, t.shape[0]), F32),
        in_specs=[
            pl.BlockSpec(memory_space=pltpu.SMEM),
            pl.BlockSpec((EB, width), lambda e: (e, 0)),
            whole(hi.shape),
            whole(lo.shape),
            whole(t.shape),
            whole(scale.shape),
        ],
        out_specs=whole((blocks, t.shape[0])),
        compiler_params=pltpu.CompilerParams(vmem_limit_bytes=VMEM_BYTES),
        cost_estimate=pl.CostEstimate(
            flops=6 * evals.size * width,
            bytes_accessed=evals.size * 2 + width * width * 6,
            transcendentals=0,
        ),
        name="scores",
    )(flags, evals, hi, lo, t, scale)


def bit_groups(n):
    bits = [1 << s for s in range(n.bit_length() - 1)]
    groups = [[b] for b in bits[:2]]
    rest = bits[2:]
    while rest:
        groups.append(rest[:2])
        rest = rest[2:]
    return groups


def send(x, mask, n):
    return lax.ppermute(x, "dp", [(i, i ^ mask) for i in range(n)])


def place_of(index, n):
    place, step = 0, n
    for group in bit_groups(n):
        size = 1 << len(group)
        step //= size
        place = place + (index // group[0]) % size * step
    return place


def all_reduce(x, n):
    groups = bit_groups(n)
    for group in groups:
        size = 1 << len(group)
        part = x.shape[0] // size
        total = x[:part]
        for q in range(1, size):
            total = total + send(x[q * part : (q + 1) * part], q * group[0], n)
        x = total
    for group in reversed(groups):
        x = jnp.concatenate([x] + [send(x, q * group[0], n) for q in range(1, 1 << len(group))])
    return x


def per_device(train_grads, eval_grads, pair_eval, pair_count, n):
    width = train_grads.shape[1]
    nb = width // B
    index = lax.axis_index("dp")
    me = place_of(index, n)[None]
    packed = local_gram(me, train_grads, n)
    packed = all_reduce(packed, n)
    hi, lo = gram_inverse(me, packed, nb, n)
    evals = lax.all_gather(eval_grads, "dp", axis=0, tiled=True)
    blocks = evals.shape[0] // EB
    squares = jnp.sum(jnp.square(train_grads.astype(F32)), axis=1)
    scale = lax.rsqrt(squares + EPSILON)[None, :]
    order, count = pair_eval[index], pair_count[index]
    hits = order[:, None] == jnp.arange(blocks, dtype=jnp.int32)[None, :]
    inside = jnp.arange(order.shape[0], dtype=jnp.int32)[:, None] < count
    flags = jnp.any(hits & inside, axis=0).astype(jnp.int32)
    return scores(flags, evals, hi, lo, train_grads, scale)


def solution(mesh):
    placed = (P(("groups", "dp"), None), P(("groups", "dp"), None), P("groups", None), P("groups"))
    return jax.shard_map(
        functools.partial(per_device, n=mesh.shape["dp"]),
        mesh=mesh,
        in_specs=placed,
        out_specs=P(None, ("groups", "dp")),
        check_vma=False,
    )
```

time: 558 us -> 157 us (0.28)
  the two profiles are of different devices: /device:TPU:21 before, /device:TPU:19 now
where the time goes in v1:
time: 157 us
  Pallas kernels  68.7 us (44%)
  waiting for transfers between devices  51.7 us (33%)
  between operations  13.5 us (9%)
  starting transfers between devices  11.4 us (7%)
  local copies, waits for them, and re-layouts  7.87 us (5%)
  other arithmetic  3.32 us (2%)
    pallas_call x1, Pallas kernels, gram_inverse(): pl.pallas_call(functools.partial(inverse_kernel, nb=nb, pieces=pieces), o...  53 us
    ppermute x10, waiting for transfers between devices, send(): return lax.ppermute(x, 'dp', [(i, i ^ mask) for i in range(n)])  51.7 us
    ppermute x10, starting transfers between devices, send(): return lax.ppermute(x, 'dp', [(i, i ^ mask) for i in range(n)])  11.4 us
    pallas_call x1, Pallas kernels, scores(): pl.pallas_call(score_kernel, grid=(blocks,), out_shape=jax.ShapeDtypeStru...  11 us
    pallas_call x1, Pallas kernels, local_gram(): pl.pallas_call(functools.partial(gram_kernel, nb=nb, pieces=pieces), out_...  4.71 us
    unnamed x14, local copies, waits for them, and re-layouts  3.52 us
  transfers between devices with their start and end apart: 11, of which 9 were waited for; matrix products, arithmetic and copies ran while one was open for 5% of the time, Pallas kernels for 34%

profile of v1, /device:TPU:19, one launch (start us, length us, event | category | flops | bytes accessed | tf_op | source)
XLA Modules:
  0.0 156.5 jit_solution(5252493923761767662)
XLA Ops:
  6.5 4.7 %local_gram.1 = f32[4608,128]{1,0:T(8,128)} custom-call(s32[1]{0:T(128)} %bitcast.1.me_ref, bf16[1024,1024]{1,0:T(8,128)(2,1)} %t_ref.3), custom_call_target="tpu_custom_call" | custom-call | flops 1073741824 | bytes 4456448 | tf_op jit(solution)/shard_map/local_gram/pallas_call | solution.py:65
  11.3 1.5 slice.33
  12.8 0.7 collective-permute-start
  13.5 2.5 %collective-permute-done = f32[2304,128]{1,0:T(8,128)S(1)} collective-permute-done((f32[2304,128]{1,0:T(8,128)S(1)}, f32[2304,128]{1,0:T(8,128)S(1)}, u32[]{:S(2)}, u32[]{:S(2)}) %collective-permute-start) | collective-permute-done | bytes 1179680 | tf_op jit(solution)/shard_map/ppermute | solution.py:279
  16.1 1.3 collective-permute-start.1
  17.4 13.3 %collective-permute-done.1 = f32[1152,128]{1,0:T(8,128)S(1)} collective-permute-done((f32[1152,128]{1,0:T(8,128)S(1)}, f32[1152,128]{1,0:T(8,128)S(1)}, u32[]{:S(2)}, u32[]{:S(2)}) %collective-permute-start.1) | collective-permute-done | bytes 589856 | tf_op jit(solution)/shard_map/ppermute | solution.py:279
  30.9 1.4 collective-permute-start.2
  32.3 1.3 collective-permute-start.4
  33.6 2.3 %collective-permute-done.2 = f32[288,128]{1,0:T(8,128)S(1)} collective-permute-done((f32[288,128]{1,0:T(8,128)S(1)}, f32[288,128]{1,0:T(8,128)S(1)}, u32[]{:S(2)}, u32[]{:S(2)}) %collective-permute-start.2) | collective-permute-done | bytes 147488 | tf_op jit(solution)/shard_map/ppermute | solution.py:279
  35.9 2.9 %collective-permute-done.3 = f32[288,128]{1,0:T(8,128)S(1)} collective-permute-done((f32[288,128]{1,0:T(8,128)S(1)}, f32[288,128]{1,0:T(8,128)S(1)}, u32[]{:S(2)}, u32[]{:S(2)}) %collective-permute-start.3) | collective-permute-done | bytes 147488 | tf_op jit(solution)/shard_map/ppermute | solution.py:279
  38.9 7.2 %collective-permute-done.4 = f32[288,128]{1,0:T(8,128)S(1)} collective-permute-done((f32[288,128]{1,0:T(8,128)S(1)}, f32[288,128]{1,0:T(8,128)S(1)}, u32[]{:S(2)}, u32[]{:S(2)}) %collective-permute-start.4) | collective-permute-done | bytes 147488 | tf_op jit(solution)/shard_map/ppermute | solution.py:279
  46.0 0.7 constant_dynamic-update-slice_fusion.4
  46.8 0.9 collective-permute-start.6
  47.7 1.7 %collective-permute-start.7 = (f32[288,128]{1,0:T(8,128)S(1)}, f32[288,128]{1,0:T(8,128)S(1)}, u32[]{:S(2)}, u32[]{:S(2)}) collective-permute-start(f32[288,128]{1,0:T(8,128)S(1)} %get-tuple-element.10), channel_id=1, source_target_pairs={{0,12},{1,13},{2,14},{3,15},{4,8},{5,9},{6,10},{7,11},{8,4},{9,5},... | collective-permute-start | bytes 442376 | tf_op jit(solution)/shard_map/ppermute | solution.py:279
  49.5 1.3 collective-permute-done.5
  50.8 1.3 collective-permute-done.6
  52.1 11.1 %collective-permute-done.7 = f32[288,128]{1,0:T(8,128)S(1)} collective-permute-done((f32[288,128]{1,0:T(8,128)S(1)}, f32[288,128]{1,0:T(8,128)S(1)}, u32[]{:S(2)}, u32[]{:S(2)}) %collective-permute-start.7) | collective-permute-done | bytes 147488 | tf_op jit(solution)/shard_map/ppermute | solution.py:279
  63.2 1.4 collective-permute-start.8
  64.6 0.7 constant_dynamic-update-slice_fusion.3
  65.3 0.7 constant_dynamic-update-slice_fusion.2
  66.0 0.7 constant_dynamic-update-slice_fusion.1
  66.7 9.7 %collective-permute-done.8 = f32[1152,128]{1,0:T(8,128)S(1)} collective-permute-done((f32[1152,128]{1,0:T(8,128)S(1)}, f32[1152,128]{1,0:T(8,128)S(1)}, u32[]{:S(2)}, u32[]{:S(2)}) %collective-permute-start.8) | collective-permute-done | bytes 589856 | tf_op jit(solution)/shard_map/ppermute | solution.py:279
  76.4 0.9 constant_dynamic-update-slice_fusion
  77.3 1.4 copy-done.3
  78.7 2.7 %collective-permute-start.9 = (f32[2304,128]{1,0:T(8,128)}, f32[2304,128]{1,0:T(8,128)S(1)}, u32[]{:S(2)}, u32[]{:S(2)}) collective-permute-start(f32[2304,128]{1,0:T(8,128)} %get-tuple-element.11), channel_id=1, source_target_pairs={{0,1},{1,0},{2,3},{3,2},{4,5},{5,4},{6,7},{7,6},{8,9},{9,8},{10,11... | collective-permute-start | bytes 3538952 | tf_op jit(solution)/shard_map/ppermute | solution.py:279
  81.4 0.6 dynamic_slice.7
  82.2 0.7 iota_compare_fusion.1
  82.9 0.5 convert_element_type.6.flag_ref
  83.9 0.6 add_rsqrt_fusion
  84.5 1.1 constant_dynamic-update-slice_fusion.5.g_ref
  85.6 53.0 %gram_inverse.1 = (bf16[1024,1024]{1,0:T(8,128)(2,1)}, bf16[1024,1024]{1,0:T(8,128)(2,1)}) custom-call(s32[1]{0:T(128)} %bitcast.1.me_ref, f32[4608,128]{1,0:T(8,128)} %constant_dynamic-update-slice_fusion.5.g_ref), custom_call_target="tpu_custom_call" | custom-call | flops 12884901888 | bytes 6553600 | tf_op jit(solution)/shard_map/gram_inverse/pallas_call | solution.py:203
  138.6 11.0 %scores.1 = f32[4,1024]{1,0:T(4,128)} custom-call(s32[4]{0:T(128)} %convert_element_type.6.flag_ref, bf16[1024,1024]{1,0:T(8,128)(2,1)} %all-gather.2.cloned.1.call-done.e_ref, bf16[1024,1024]{1,0:T(8,128)(2,1)} %get-tuple-element.7.hi_ref, bf16[1024,1024]{1,0:T(8,128)(2,1)} %get-tuple-element.8.lo_ref, bf16[1024,1024]{1,0:T(8,128)(2,1)} %t_ref.3, ...), custom_call_target="tpu_custom_call" | custom-call | flops 6442450944 | bytes 8388608 | tf_op jit(solution)/shard_map/scores/pallas_call | solution.py:245
  (24 shorter events, 1.2 us)
Async XLA Ops:
  6.5 75.4 %copy-start = (s32[16,4]{0,1:T(4,128)S(1)}, s32[16,4]{0,1:T(4,128)}, u32[]{:S(2)}) copy-start(s32[16,4]{0,1:T(4,128)} %param.6) | copy-start | bytes 772
  6.5 132.1 %all-gather.2.cloned.1.call-start = ((), (), s32[]{:S(2)}) async-start(), calls=%async_computation | async-start | bytes 2228224 | tf_op jit(solution)/shard_map/all_gather | solution.py:313
  11.2 4.7 %copy-start.1 = (f32[4608,128]{1,0:T(8,128)S(1)}, f32[4608,128]{1,0:T(8,128)}, u32[]{:S(2)}) copy-start(f32[4608,128]{1,0:T(8,128)} %local_gram.1) | copy-start | bytes 7077892
  12.8 3.2 %collective-permute-start = (f32[2304,128]{1,0:T(8,128)S(1)}, f32[2304,128]{1,0:T(8,128)S(1)}, u32[]{:S(2)}, u32[]{:S(2)}) collective-permute-start(f32[2304,128]{1,0:T(8,128)S(1)} %slice.33), channel_id=1, source_target_pairs={{0,1},{1,0},{2,3},{3,2},{4,5},{5,4},{6,7},{7,6},{8,9},{9,8},{10,11... | collective-permute-start | bytes 3538952 | tf_op jit(solution)/shard_map/ppermute | solution.py:279
  16.1 14.6 %collective-permute-start.1 = (f32[1152,128]{1,0:T(8,128)S(1)}, f32[1152,128]{1,0:T(8,128)S(1)}, u32[]{:S(2)}, u32[]{:S(2)}) collective-permute-start(f32[1152,128]{1,0:T(8,128)S(1)} %slice.35), channel_id=1, source_target_pairs={{0,2},{1,3},{2,0},{3,1},{4,6},{5,7},{6,4},{7,5},{8,10},{9,11},{10,... | collective-permute-start | bytes 1769480 | tf_op jit(solution)/shard_map/ppermute | solution.py:279
  30.9 5.0 %collective-permute-start.2 = (f32[288,128]{1,0:T(8,128)S(1)}, f32[288,128]{1,0:T(8,128)S(1)}, u32[]{:S(2)}, u32[]{:S(2)}) collective-permute-start(f32[288,128]{1,0:T(8,128)S(1)} %get-tuple-element.13), channel_id=1, source_target_pairs={{0,4},{1,5},{2,6},{3,7},{4,0},{5,1},{6,2},{7,3},{8,12},{9,13},{10,... | collective-permute-start | bytes 442376 | tf_op jit(solution)/shard_map/ppermute | solution.py:279
  32.2 6.6 %collective-permute-start.3 = (f32[288,128]{1,0:T(8,128)S(1)}, f32[288,128]{1,0:T(8,128)S(1)}, u32[]{:S(2)}, u32[]{:S(2)}) collective-permute-start(f32[288,128]{1,0:T(8,128)S(1)} %get-tuple-element.15), channel_id=1, source_target_pairs={{0,8},{1,9},{2,10},{3,11},{4,12},{5,13},{6,14},{7,15},{8,0},{9,1},... | collective-permute-start | bytes 442376 | tf_op jit(solution)/shard_map/ppermute | solution.py:279
  32.3 13.7 %collective-permute-start.4 = (f32[288,128]{1,0:T(8,128)S(1)}, f32[288,128]{1,0:T(8,128)S(1)}, u32[]{:S(2)}, u32[]{:S(2)}) collective-permute-start(f32[288,128]{1,0:T(8,128)S(1)} %get-tuple-element.14), channel_id=1, source_target_pairs={{0,12},{1,13},{2,14},{3,15},{4,8},{5,9},{6,10},{7,11},{8,4},{9,5},... | collective-permute-start | bytes 442376 | tf_op jit(solution)/shard_map/ppermute | solution.py:279
  46.8 4.0 %collective-permute-start.5 = (f32[288,128]{1,0:T(8,128)S(1)}, f32[288,128]{1,0:T(8,128)S(1)}, u32[]{:S(2)}, u32[]{:S(2)}) collective-permute-start(f32[288,128]{1,0:T(8,128)S(1)} %get-tuple-element.10), channel_id=1, source_target_pairs={{0,4},{1,5},{2,6},{3,7},{4,0},{5,1},{6,2},{7,3},{8,12},{9,13},{10,... | collective-permute-start | bytes 442376 | tf_op jit(solution)/shard_map/ppermute | solution.py:279
  46.8 5.3 %collective-permute-start.6 = (f32[288,128]{1,0:T(8,128)S(1)}, f32[288,128]{1,0:T(8,128)S(1)}, u32[]{:S(2)}, u32[]{:S(2)}) collective-permute-start(f32[288,128]{1,0:T(8,128)S(1)} %get-tuple-element.10), channel_id=1, source_target_pairs={{0,8},{1,9},{2,10},{3,11},{4,12},{5,13},{6,14},{7,15},{8,0},{9,1},... | collective-permute-start | bytes 442376 | tf_op jit(solution)/shard_map/ppermute | solution.py:279
  47.7 15.5 %collective-permute-start.7 = (f32[288,128]{1,0:T(8,128)S(1)}, f32[288,128]{1,0:T(8,128)S(1)}, u32[]{:S(2)}, u32[]{:S(2)}) collective-permute-start(f32[288,128]{1,0:T(8,128)S(1)} %get-tuple-element.10), channel_id=1, source_target_pairs={{0,12},{1,13},{2,14},{3,15},{4,8},{5,9},{6,10},{7,11},{8,4},{9,5},... | collective-permute-start | bytes 442376 | tf_op jit(solution)/shard_map/ppermute | solution.py:279
  49.4 32.0 %copy-start.4 = (s32[16]{0:T(128)S(1)}, s32[16]{0:T(128)}, u32[]{:S(2)}) copy-start(s32[16]{0:T(128)} %param.7) | copy-start | bytes 196
  49.4 34.0 %copy-start.2 = (bf16[1024,1024]{1,0:T(8,128)(2,1)S(1)}, bf16[1024,1024]{1,0:T(8,128)(2,1)}, u32[]{:S(2)}) copy-start(bf16[1024,1024]{1,0:T(8,128)(2,1)} %t_ref.3) | copy-start | bytes 6291460
  63.2 13.1 %collective-permute-start.8 = (f32[1152,128]{1,0:T(8,128)S(1)}, f32[1152,128]{1,0:T(8,128)S(1)}, u32[]{:S(2)}, u32[]{:S(2)}) collective-permute-start(f32[1152,128]{1,0:T(8,128)S(1)} %pad_maximum_fusion), channel_id=1, source_target_pairs={{0,2},{1,3},{2,0},{3,1},{4,6},{5,7},{6,4},{7,5},{8,10},{9,11},{10,... | collective-permute-start | bytes 1769480 | tf_op jit(solution)/shard_map/ppermute | solution.py:279
  77.3 1.4 copy-start.3
  78.7 5.8 %collective-permute-start.9 = (f32[2304,128]{1,0:T(8,128)}, f32[2304,128]{1,0:T(8,128)S(1)}, u32[]{:S(2)}, u32[]{:S(2)}) collective-permute-start(f32[2304,128]{1,0:T(8,128)} %get-tuple-element.11), channel_id=1, source_target_pairs={{0,1},{1,0},{2,3},{3,2},{4,5},{5,4},{6,7},{7,6},{8,9},{9,8},{10,11... | collective-permute-start | bytes 3538952 | tf_op jit(solution)/shard_map/ppermute | solution.py:279
Sparse Core Ops, SparseCore 0:
  49.6 43.1 all-gather.1

commit v2 on v1

v2 whole, which is shorter than its diff:
```python
import functools

import jax
import jax.numpy as jnp
from jax import lax
from jax.experimental import pallas as pl
from jax.experimental.pallas import tpu as pltpu
from jax.sharding import PartitionSpec as P

EB = 256
DAMPING = 0.1
EPSILON = 1e-06
B = 128
F32, BF16 = jnp.float32, jnp.bfloat16
NT = (((1,), (1,)), ((), ()))
NN = (((1,), (0,)), ((), ()))
TN = (((0,), (0,)), ((), ()))
VMEM_BYTES = 56 * 1024 * 1024


def dot(a, b, dims):
    return lax.dot_general(a, b, dims, preferred_element_type=F32)


def slab_offset(j, nb):
    return B * (j * nb - j * (j - 1) // 2)


def split3(x):
    hi = x.astype(BF16)
    rest = x - hi.astype(F32)
    mid = rest.astype(BF16)
    lo = (rest - mid.astype(F32)).astype(BF16)
    return hi, mid, lo


def left_parts(x):
    h, m, l = split3(x)
    return jnp.concatenate([h, h, m, m, h, l], axis=1)


def right_parts(x, axis=1):
    h, m, l = split3(x)
    return jnp.concatenate([h, m, h, m, l, h], axis=axis)


def chunk_plan(nb, pieces):
    cut = max(nb // 4, 1)
    plan = []
    for first, last in ((0, cut), (cut, nb)):
        start, stop = slab_offset(first, nb), slab_offset(last, nb)
        rows = -(-(stop - start) // (8 * pieces)) * 8
        plan.append((first, last, start, rows))
    return plan


def gram_kernel(me_ref, t_ref, *refs, nb, pieces):
    width = nb * B
    plan = chunk_plan(nb, pieces)
    outs, packs = refs[: 2 * len(plan)], refs[2 * len(plan) :]

    def chunk_of(j):
        return next(c for c, p in enumerate(plan) if p[0] <= j < p[1])

    for J in range(nb // 2):
        c0 = 2 * B * J
        g = dot(t_ref[:, c0:], t_ref[:, c0 : c0 + 2 * B], TN)
        for h in range(2):
            j = 2 * J + h
            c = chunk_of(j)
            o = slab_offset(j, nb) - plan[c][2]
            packs[c][o : o + width - B * j, :] = g[B * h :, B * h : B * h + B]
    me = me_ref[0]
    half = pieces // 2
    for c, (first, last, start, rows) in enumerate(plan):
        used = slab_offset(last, nb) - start
        if used < pieces * rows:
            packs[c][used:, :] = jnp.zeros((pieces * rows - used, B), F32)
        for q in range(pieces):
            at = pl.multiple_of((me ^ q) * rows, 8)
            out = outs[2 * c + q // half]
            q = q % half
            out[q * rows : (q + 1) * rows, :] = packs[c][pl.ds(at, rows), :]


def local_gram(me, t, pieces):
    nb = t.shape[1] // B
    plan = chunk_plan(nb, pieces)
    halves = [jax.ShapeDtypeStruct((pieces // 2 * p[3], B), F32) for p in plan for _ in range(2)]
    return pl.pallas_call(
        functools.partial(gram_kernel, nb=nb, pieces=pieces),
        out_shape=halves,
        in_specs=[
            pl.BlockSpec(memory_space=pltpu.SMEM),
            pl.BlockSpec(memory_space=pltpu.VMEM),
        ],
        out_specs=[pl.BlockSpec(memory_space=pltpu.VMEM) for _ in halves],
        scratch_shapes=[pltpu.VMEM((pieces * p[3], B), F32) for p in plan],
        compiler_params=pltpu.CompilerParams(vmem_limit_bytes=VMEM_BYTES),
        cost_estimate=pl.CostEstimate(
            flops=t.shape[0] * t.shape[1] * t.shape[1],
            bytes_accessed=t.size * 2 + sum(h.size for h in halves) * 4,
            transcendentals=0,
        ),
        name="local_gram",
    )(me, t)


def reduce_rows(S, R):
    S, R = [list(row) for row in S], list(R)

    def pivot(j, rc):
        s = {k: S[j][k] * rc for k in range(j + 1, 8)}
        row = R[j] * rc
        for i in range(8):
            if i == j:
                continue
            c = S[i][j] if i < j else S[j][i]
            for k in range(max(i, j + 1), 8):
                S[i][k] = S[i][k] - c * s[k]
            R[i] = R[i] - c * row
        for k in s:
            S[j][k] = s[k]
        R[j] = row

    for j in range(0, 8, 2):
        a, b, d = S[j][j], S[j][j + 1], S[j + 1][j + 1]
        rd = 1.0 / (a * d - b * b)
        pivot(j, 1.0 / a)
        pivot(j + 1, a * rd)
    return R


def invert_block(M, spread):
    M = list(M)
    full = (8, B)
    lane = lax.broadcasted_iota(jnp.int32, full, 1)
    sub = lax.broadcasted_iota(jnp.int32, full, 0)
    n = len(M)
    for b in range(n):
        k0 = 8 * b
        columns = lambda V: [jnp.broadcast_to(V[:, k0 + k : k0 + k + 1], full) for k in range(8)]
        base = 64 * (b % 2)
        for j, column in enumerate(columns(M[b])):
            spread[base + 8 * j : base + 8 * j + 8, :] = column
        S = [
            [None] * i + [spread[pl.ds(base + 8 * j + i, 8, stride=0), :] for j in range(i, 8)]
            for i in range(8)
        ]
        inside = (lane >= k0) & (lane < k0 + 8)
        R = [
            jnp.where(
                inside,
                jnp.where(lane == k0 + i, 1.0, 0.0).astype(F32),
                jnp.broadcast_to(M[b][i : i + 1, :], full),
            )
            for i in range(8)
        ]
        R = reduce_rows(S, R)
        for q in range(1, n + 1):
            t = (b + q) % n
            if t == b:
                x = R[0]
                for i in range(1, 8):
                    x = jnp.where(sub == i, R[i], x)
            else:
                c = columns(M[t])
                x, y = jnp.where(inside, 0.0, M[t]) - c[0] * R[0], c[1] * R[1]
                for k in (2, 4, 6):
                    x, y = x - c[k] * R[k], y + c[k + 1] * R[k + 1]
                x = x - y
            M[t] = x
    return M


def inverse_kernel(me_ref, *refs, nb, pieces):
    width = nb * B
    plan = chunk_plan(nb, pieces)
    count = len(plan)
    parts, (hi_ref, lo_ref), packs = refs[: 2 * count], refs[2 * count : 2 * count + 2], refs[2 * count + 2 : 3 * count + 2]
    A, D, inv, spread, W, WL, CL, CR = refs[3 * count + 2 :]
    me = me_ref[0]
    half = pieces // 2
    for c, (_, _, _, rows) in enumerate(plan):
        for q in range(pieces):
            to = pl.multiple_of((me ^ q) * rows, 8)
            p = q % half
            packs[c][pl.ds(to, rows), :] = parts[2 * c + q // half][p * rows : (p + 1) * rows, :]

    def column(j):
        c = next(c for c, p in enumerate(plan) if p[0] <= j < p[1])
        return packs[c], slab_offset(j, nb) - plan[c][2]

    eye = lax.broadcasted_iota(jnp.int32, (B, B), 0) == lax.broadcasted_iota(
        jnp.int32, (B, B), 1
    )
    diag = jnp.zeros((B, B), F32)
    for j in range(nb):
        pack, o = column(j)
        diag = diag + jnp.where(eye, pack[o : o + B, :], 0.0)
    trace = jnp.sum(jnp.sum(diag, axis=1, keepdims=True), axis=0, keepdims=True)
    scale = jnp.broadcast_to(width / trace, (1, B))
    damp = jnp.where(eye, DAMPING, 0.0).astype(F32)
    for j in range(nb):
        pack, o = column(j)
        A[j, B * j : B * j + B, :] = pack[o : o + B, :] * scale + damp
        if j + 1 < nb:
            A[j, B * j + B :, :] = pack[o + B : o + width - B * j, :] * scale
    MC = 256

    def split_column(k):
        for i in range(nb):
            x = A[k, B * i : B * i + B, :]
            x = jnp.where(k == i, jnp.zeros_like(x), x)
            CL[B * i : B * i + B, :] = left_parts(x)
            CR[B * i : B * i + B, :] = right_parts(x)

    def eliminate(k):
        pivot = inv[...]
        right = right_parts(pivot, axis=0)
        for i in range(nb):
            w = dot(CL[B * i : B * i + B, :], right, NN)
            w = jnp.where(k == i, -pivot, w)
            W[B * i : B * i + B, :] = w
            WL[B * i : B * i + B, :] = left_parts(w)
        for J in range(nb // 2):
            cols = CR[2 * B * J : 2 * B * (J + 1), :]
            for r in range(0, width, MC):
                u = dot(WL[r : r + MC, :], cols, NT)
                for h in range(2):
                    for q in range(0, MC, B):
                        at = slice(r + q, r + q + B)
                        x = A[2 * J + h, at, :]
                        x = jnp.where(k == (r + q) // B, jnp.zeros_like(x), x)
                        A[2 * J + h, at, :] = x - u[q : q + B, h * B : h * B + B]
        A[k] = W[...]

    def invert():
        return jnp.concatenate(
            invert_block([D[8 * t : 8 * t + 8, :] for t in range(B // 8)], spread)
        )

    def next_pivot(k):
        at = pl.ds(pl.multiple_of(k * B, B), B)
        w = dot(CL[at, :], right_parts(inv[...], axis=0), NN)
        D[...] = A[k, at, :] - dot(left_parts(w), CR[at, :], NT)

    D[...] = A[0, :B, :]
    split_column(0)
    inv[...] = invert()
    next_pivot(1)

    def step(k, carry):
        after = invert()
        eliminate(k)
        split_column(k + 1)
        inv[...] = after
        next_pivot(jnp.minimum(k + 2, nb - 1))
        return carry

    lax.fori_loop(0, nb - 1, step, 0)
    eliminate(nb - 1)
    for j in range(nb):
        x = -A[j]
        hi = x.astype(BF16)
        hi_ref[:, B * j : B * j + B] = hi
        lo_ref[:, B * j : B * j + B] = (x - hi.astype(F32)).astype(BF16)


def gram_inverse(me, parts, nb, pieces):
    width = nb * B
    out = jax.ShapeDtypeStruct((width, width), BF16)
    return pl.pallas_call(
        functools.partial(inverse_kernel, nb=nb, pieces=pieces),
        out_shape=(out, out),
        in_specs=[pl.BlockSpec(memory_space=pltpu.SMEM)]
        + [pl.BlockSpec(memory_space=pltpu.VMEM) for _ in parts],
        out_specs=(pl.BlockSpec(memory_space=pltpu.VMEM),) * 2,
        scratch_shapes=[pltpu.VMEM((pieces * p[3], B), F32) for p in chunk_plan(nb, pieces)]
        + [
            pltpu.VMEM((nb, width, B), F32),
            pltpu.VMEM((B, B), F32),
            pltpu.VMEM((B, B), F32),
            pltpu.VMEM((B, B), F32),
            pltpu.VMEM((width, B), F32),
            pltpu.VMEM((width, 6 * B), BF16),
            pltpu.VMEM((width, 6 * B), BF16),
            pltpu.VMEM((width, 6 * B), BF16),
        ],
        compiler_params=pltpu.CompilerParams(vmem_limit_bytes=VMEM_BYTES),
        cost_estimate=pl.CostEstimate(
            flops=12 * width**3, bytes_accessed=width * width * 8, transcendentals=0
        ),
        name="gram_inverse",
    )(me, *parts)


def score_kernel(me_ref, flag_ref, hi_ref, lo_ref, t_ref, scale_ref, *refs, rows):
    parts, out_ref, evals = refs[:-2], refs[-2], refs[-1]
    e = pl.program_id(0)

    @pl.when(e == 0)
    def _():
        for q2, part in enumerate(parts):
            for q in range(part.shape[0] // rows):
                owner = me_ref[0] ^ (q * len(parts) + q2)
                to = pl.multiple_of(owner * rows, 16)
                evals[pl.ds(to, rows), :] = part[q * rows : (q + 1) * rows, :]

    @pl.when(flag_ref[e] > 0)
    def _():
        block = evals[pl.ds(pl.multiple_of(e * EB, EB), EB), :]
        pre = (dot(block, hi_ref[...], NN) + dot(block, lo_ref[...], NN)).astype(BF16)
        score = dot(pre, t_ref[...], NT)
        out_ref[pl.ds(e, 1), :] = jnp.max(score, axis=0, keepdims=True) * scale_ref[...]

    @pl.when(flag_ref[e] <= 0)
    def _():
        out_ref[pl.ds(e, 1), :] = jnp.zeros((1, out_ref.shape[1]), F32)


def scores(index, flags, parts, rows, hi, lo, t, scale):
    total = sum(p.shape[0] for p in parts)
    blocks = total // EB
    width = t.shape[1]
    whole = lambda shape: pl.BlockSpec(shape, lambda e: (0, 0))
    smem = pl.BlockSpec(memory_space=pltpu.SMEM)
    operands = (hi, lo, t, scale) + tuple(parts)
    return pl.pallas_call(
        functools.partial(score_kernel, rows=rows),
        grid=(blocks,),
        out_shape=jax.ShapeDtypeStruct((blocks, t.shape[0]), F32),
        in_specs=[smem, smem] + [whole(x.shape) for x in operands],
        out_specs=whole((blocks, t.shape[0])),
        scratch_shapes=[pltpu.VMEM((total, width), BF16)],
        compiler_params=pltpu.CompilerParams(vmem_limit_bytes=VMEM_BYTES),
        cost_estimate=pl.CostEstimate(
            flops=6 * total * width * width,
            bytes_accessed=total * width * 2 + width * width * 6,
            transcendentals=0,
        ),
        name="scores",
    )(index, flags, *operands)


def bit_groups(n):
    bits = [1 << s for s in range(n.bit_length() - 1)]
    groups = [[b] for b in bits[:2]]
    rest = bits[2:]
    while rest:
        groups.append(rest[:2])
        rest = rest[2:]
    return groups


def send(x, mask, n):
    return lax.ppermute(x, "dp", [(i, i ^ mask) for i in range(n)])


def place_of(index, n):
    place, step = 0, n
    for group in bit_groups(n):
        size = 1 << len(group)
        step //= size
        place = place + (index // group[0]) % size * step
    return place


def spread_out(x, group, n):
    return [x] + [send(x, q * group[0], n) for q in range(1, 1 << len(group))]


def all_reduce(chunks, n):
    groups = bit_groups(n)
    chunks = [keep + send(other, groups[0][0], n) for keep, other in chunks]
    for group in groups[1:]:
        size = 1 << len(group)
        after = []
        for x in chunks:
            part = x.shape[0] // size
            total = x[:part]
            for q in range(1, size):
                total = total + send(x[q * part : (q + 1) * part], q * group[0], n)
            after.append(total)
        chunks = after
    for group in reversed(groups[1:]):
        chunks = [jnp.concatenate(spread_out(x, group, n)) for x in chunks]
    return [(x, send(x, groups[0][0], n)) for x in chunks]


def per_device(train_grads, eval_grads, pair_eval, pair_count, n):
    width = train_grads.shape[1]
    nb = width // B
    index = lax.axis_index("dp")
    evals = eval_grads
    for group in bit_groups(n)[2:]:
        evals = jnp.concatenate(spread_out(evals, group, n))
    me = place_of(index, n)[None]
    halves = local_gram(me, train_grads, n)
    chunks = all_reduce(list(zip(halves[::2], halves[1::2])), n)
    chunks, evals = lax.optimization_barrier((chunks, evals))
    parts = spread_out(evals, [1, 2], n)
    hi, lo = gram_inverse(me, [x for pair in chunks for x in pair], nb, n)
    blocks = eval_grads.shape[0] * n // EB
    squares = jnp.sum(jnp.square(train_grads.astype(F32)), axis=1)
    scale = lax.rsqrt(squares + EPSILON)[None, :]
    order, count = pair_eval[index], pair_count[index]
    hits = order[:, None] == jnp.arange(blocks, dtype=jnp.int32)[None, :]
    inside = jnp.arange(order.shape[0], dtype=jnp.int32)[:, None] < count
    flags = jnp.any(hits & inside, axis=0).astype(jnp.int32)
    return scores(index[None], flags, parts, eval_grads.shape[0], hi, lo, train_grads, scale)


def solution(mesh):
    placed = (P(("groups", "dp"), None), P(("groups", "dp"), None), P("groups", None), P("groups"))
    return jax.shard_map(
        functools.partial(per_device, n=mesh.shape["dp"]),
        mesh=mesh,
        in_specs=placed,
        out_specs=P(None, ("groups", "dp")),
        check_vma=False,
    )
```

time: 157 us -> 133 us (0.85)
  the two profiles are of different devices: /device:TPU:19 before, /device:TPU:11 now
where the time goes in v2:
time: 133 us; the launch traced here: 132 us
  Pallas kernels  61.9 us (47%)
  starting transfers between devices  34.4 us (26%)
  waiting for transfers between devices  30 us (23%)
  other arithmetic  3.78 us (3%)
  local copies, waits for them, and re-layouts  2.08 us (2%)
    pallas_call x1, Pallas kernels, gram_inverse(): pl.pallas_call(functools.partial(inverse_kernel, nb=nb, pieces=pieces), o...  45.9 us
    ppermute x26, starting transfers between devices, send(): return lax.ppermute(x, 'dp', [(i, i ^ mask) for i in range(n)])  34.4 us
    ppermute x26, waiting for transfers between devices, send(): return lax.ppermute(x, 'dp', [(i, i ^ mask) for i in range(n)])  30 us
    pallas_call x1, Pallas kernels, scores(): pl.pallas_call(functools.partial(score_kernel, rows=rows), grid=(blocks,)...  11.5 us
    pallas_call x1, Pallas kernels, local_gram(): pl.pallas_call(functools.partial(gram_kernel, nb=nb, pieces=pieces), out_...  4.42 us
  transfers between devices with their start and end apart: 26, of which 14 were waited for; matrix products, arithmetic and copies ran while one was open for 3% of the time, Pallas kernels for 35%

profile of v2, /device:TPU:11, one launch (start us, length us, event | category | flops | bytes accessed | tf_op | source)
XLA Modules:
  0.0 132.3 jit_solution(17522634622904721698)
XLA Ops:
  0.0 4.4 %local_gram.1 = (f32[960,128]{1,0:T(8,128)}, f32[960,128]{1,0:T(8,128)}, f32[1344,128]{1,0:T(8,128)}, f32[1344,128]{1,0:T(8,128)}) custom-call(s32[1]{0:T(128)} %bitcast.2.me_ref, bf16[1024,1024]{1,0:T(8,128)(2,1)} %t_ref.3), custom_call_target="tpu_custom_call" | custom-call | flops 1073741824 | bytes 4456448 | tf_op jit(solution)/shard_map/local_gram/pallas_call | solution.py:90
  4.4 0.7 collective-permute-start
  5.1 1.7 %collective-permute-done = f32[960,128]{1,0:T(8,128)S(1)} collective-permute-done((f32[960,128]{1,0:T(8,128)}, f32[960,128]{1,0:T(8,128)S(1)}, u32[]{:S(2)}, u32[]{:S(2)}) %collective-permute-start) | collective-permute-done | bytes 491552 | tf_op jit(solution)/shard_map/ppermute | solution.py:357
  6.8 1.1 add.73
  7.9 1.3 collective-permute-start.1
  10.8 4.3 %collective-permute-done.1 = f32[480,128]{1,0:T(8,128)S(1)} collective-permute-done((f32[480,128]{1,0:T(8,128)S(1)}, f32[480,128]{1,0:T(8,128)S(1)}, u32[]{:S(2)}, u32[]{:S(2)}) %collective-permute-start.1) | collective-permute-done | bytes 245792 | tf_op jit(solution)/shard_map/ppermute | solution.py:357
  15.5 2.3 %collective-permute-start.3 = (f32[120,128]{1,0:T(8,128)S(1)}, f32[120,128]{1,0:T(8,128)S(1)}, u32[]{:S(2)}, u32[]{:S(2)}) collective-permute-start(f32[120,128]{1,0:T(8,128)S(1)} %get-tuple-element.36), channel_id=1, source_target_pairs={{0,8},{1,9},{2,10},{3,11},{4,12},{5,13},{6,14},{7,15},{8,0},{9,1},... | collective-permute-start | bytes 184328 | tf_op jit(solution)/shard_map/ppermute | solution.py:357
  18.7 1.3 collective-permute-start.11
  20.1 0.7 collective-permute-done.4
  20.9 3.1 %collective-permute-start.5 = (f32[120,128]{1,0:T(8,128)S(1)}, f32[120,128]{1,0:T(8,128)S(1)}, u32[]{:S(2)}, u32[]{:S(2)}) collective-permute-start(f32[120,128]{1,0:T(8,128)S(1)} %get-tuple-element.30), channel_id=1, source_target_pairs={{0,4},{1,5},{2,6},{3,7},{4,0},{5,1},{6,2},{7,3},{8,12},{9,13},{10,... | collective-permute-start | bytes 184328 | tf_op jit(solution)/shard_map/ppermute | solution.py:357
  24.2 1.1 collective-permute-start.7
  26.0 1.9 %collective-permute-start.21 = (bf16[64,1024]{1,0:T(8,128)(2,1)S(1)}, bf16[64,1024]{1,0:T(8,128)(2,1)S(1)}, u32[]{:S(2)}, u32[]{:S(2)}) collective-permute-start(bf16[64,1024]{1,0:T(8,128)(2,1)S(1)} %copy-done.4), channel_id=1, source_target_pairs={{0,8},{1,9},{2,10},{3,11},{4,12},{5,13},{6,14},{7,15},{8,0},{9,1},... | collective-permute-start | bytes 393224 | tf_op jit(solution)/shard_map/ppermute | solution.py:357
  28.1 1.1 collective-permute-done.7
  29.3 0.9 collective-permute-start.12
  30.2 1.6 %collective-permute-start.13 = (f32[168,128]{1,0:T(8,128)S(1)}, f32[168,128]{1,0:T(8,128)S(1)}, u32[]{:S(2)}, u32[]{:S(2)}) collective-permute-start(f32[168,128]{1,0:T(8,128)S(1)} %get-tuple-element.33), channel_id=1, source_target_pairs={{0,8},{1,9},{2,10},{3,11},{4,12},{5,13},{6,14},{7,15},{8,0},{9,1},... | collective-permute-start | bytes 258056 | tf_op jit(solution)/shard_map/ppermute | solution.py:357
  32.0 1.4 %collective-permute-done.12 = f32[168,128]{1,0:T(8,128)S(1)} collective-permute-done((f32[168,128]{1,0:T(8,128)S(1)}, f32[168,128]{1,0:T(8,128)S(1)}, u32[]{:S(2)}, u32[]{:S(2)}) %collective-permute-start.12) | collective-permute-done | bytes 86048 | tf_op jit(solution)/shard_map/ppermute | solution.py:357
  33.4 5.9 %collective-permute-done.13 = f32[168,128]{1,0:T(8,128)S(1)} collective-permute-done((f32[168,128]{1,0:T(8,128)S(1)}, f32[168,128]{1,0:T(8,128)S(1)}, u32[]{:S(2)}, u32[]{:S(2)}) %collective-permute-start.13) | collective-permute-done | bytes 86048 | tf_op jit(solution)/shard_map/ppermute | solution.py:357
  39.3 2.1 %collective-permute-done.14 = f32[168,128]{1,0:T(8,128)S(1)} collective-permute-done((f32[168,128]{1,0:T(8,128)S(1)}, f32[168,128]{1,0:T(8,128)S(1)}, u32[]{:S(2)}, u32[]{:S(2)}) %collective-permute-start.14) | collective-permute-done | bytes 86048 | tf_op jit(solution)/shard_map/ppermute | solution.py:357
  41.8 2.0 %collective-permute-start.16 = (f32[168,128]{1,0:T(8,128)S(1)}, f32[168,128]{1,0:T(8,128)S(1)}, u32[]{:S(2)}, u32[]{:S(2)}) collective-permute-start(f32[168,128]{1,0:T(8,128)S(1)} %get-tuple-element.28), channel_id=1, source_target_pairs={{0,8},{1,9},{2,10},{3,11},{4,12},{5,13},{6,14},{7,15},{8,0},{9,1},... | collective-permute-start | bytes 258056 | tf_op jit(solution)/shard_map/ppermute | solution.py:357
  44.1 1.7 %collective-permute-done.15 = f32[168,128]{1,0:T(8,128)S(1)} collective-permute-done((f32[168,128]{1,0:T(8,128)S(1)}, f32[168,128]{1,0:T(8,128)S(1)}, u32[]{:S(2)}, u32[]{:S(2)}) %collective-permute-start.15) | collective-permute-done | bytes 86048 | tf_op jit(solution)/shard_map/ppermute | solution.py:357
  45.8 1.0 collective-permute-start.22
  46.8 3.1 %collective-permute-done.16 = f32[168,128]{1,0:T(8,128)S(1)} collective-permute-done((f32[168,128]{1,0:T(8,128)S(1)}, f32[168,128]{1,0:T(8,128)S(1)}, u32[]{:S(2)}, u32[]{:S(2)}) %collective-permute-start.16) | collective-permute-done | bytes 86048 | tf_op jit(solution)/shard_map/ppermute | solution.py:357
  49.9 1.2 collective-permute-start.8
  51.2 0.7 collective-permute-done.17
  51.9 1.3 collective-permute-start.18
  53.3 5.7 %collective-permute-done.18 = f32[672,128]{1,0:T(8,128)S(1)} collective-permute-done((f32[672,128]{1,0:T(8,128)S(1)}, f32[672,128]{1,0:T(8,128)S(1)}, u32[]{:S(2)}, u32[]{:S(2)}) %collective-permute-start.18) | collective-permute-done | bytes 344096 | tf_op jit(solution)/shard_map/ppermute | solution.py:357
  59.0 10.1 %collective-permute-start.19 = (f32[1344,128]{1,0:T(8,128)S(1)}, f32[1344,128]{1,0:T(8,128)S(1)}, u32[]{:S(2)}, u32[]{:S(2)}) collective-permute-start(f32[1344,128]{1,0:T(8,128)S(1)} %constant_dynamic-update-slice_fusion.5.refs_2_), channel_id=1, source_target_pairs={{0,1},{1,0},{2,3},{3,2},{4,5},{5,4},{6,7},{7,6},{8,9},{9,8},{10,11... | collective-permute-start | bytes 2064392 | tf_op jit(solution)/shard_map/ppermute | solution.py:357
  70.4 1.2 collective-permute-done.9.refs_1_
  72.0 1.3 collective-permute-start.24
  73.7 45.9 %gram_inverse.1 = (bf16[1024,1024]{1,0:T(8,128)(2,1)}, bf16[1024,1024]{1,0:T(8,128)(2,1)}) custom-call(s32[1]{0:T(128)} %bitcast.2.me_ref, f32[960,128]{1,0:T(8,128)} %copy-done.6, f32[960,128]{1,0:T(8,128)} %copy-done.11, f32[1344,128]{1,0:T(8,128)} %copy-done.5, f32[1344,128]{1,0:T(8,128)} %copy-done.7), custom_call_target="tpu_custom_call" | custom-call | flops 12884901888 | bytes 8388608 | tf_op jit(solution)/shard_map/gram_inverse/pallas_call | solution.py:273
  119.7 0.8 copy-done.8
  120.8 11.5 %scores.1 = f32[4,1024]{1,0:T(4,128)} custom-call(s32[1]{0:T(128)} %bitcast.me_ref, s32[4]{0:T(128)} %convert_element_type.6.flag_ref, bf16[1024,1024]{1,0:T(8,128)(2,1)} %get-tuple-element.24.hi_ref, bf16[1024,1024]{1,0:T(8,128)(2,1)} %get-tuple-element.25.lo_ref, bf16[1024,1024]{1,0:T(8,128)(2,1)} %t_ref.3, f32[1,1024]{1,0:T(1,128)} %bitcast.4, ...), custom_call_target="tpu_custom_call" | custom-call | flops 6442450944 | bytes 8388608 | tf_op jit(solution)/shard_map/scores/pallas_call | solution.py:329
  (77 shorter events, 7.8 us)
Async XLA Ops:
  0.0 10.7 %copy-start = (s32[16,4]{0,1:T(4,128)S(1)}, s32[16,4]{0,1:T(4,128)}, u32[]{:S(2)}) copy-start(s32[16,4]{0,1:T(4,128)} %param.6) | copy-start | bytes 772
  0.0 10.1 %copy-start.12 = (s32[16]{0:T(128)S(1)}, s32[16]{0:T(128)}, u32[]{:S(2)}) copy-start(s32[16]{0:T(128)} %param.7) | copy-start | bytes 196
  4.4 14.2 %copy-start.2 = (f32[1344,128]{1,0:T(8,128)S(1)}, f32[1344,128]{1,0:T(8,128)}, u32[]{:S(2)}) copy-start(f32[1344,128]{1,0:T(8,128)} %get-tuple-element.18) | copy-start | bytes 2064388
  4.4 2.4 %collective-permute-start = (f32[960,128]{1,0:T(8,128)}, f32[960,128]{1,0:T(8,128)S(1)}, u32[]{:S(2)}, u32[]{:S(2)}) collective-permute-start(f32[960,128]{1,0:T(8,128)} %get-tuple-element.17), channel_id=1, source_target_pairs={{0,1},{1,0},{2,3},{3,2},{4,5},{5,4},{6,7},{7,6},{8,9},{9,8},{10,11... | collective-permute-start | bytes 1474568 | tf_op jit(solution)/shard_map/ppermute | solution.py:357
  7.9 7.2 %collective-permute-start.1 = (f32[480,128]{1,0:T(8,128)S(1)}, f32[480,128]{1,0:T(8,128)S(1)}, u32[]{:S(2)}, u32[]{:S(2)}) collective-permute-start(f32[480,128]{1,0:T(8,128)S(1)} %slice.49), channel_id=1, source_target_pairs={{0,2},{1,3},{2,0},{3,1},{4,6},{5,7},{6,4},{7,5},{8,10},{9,11},{10,... | collective-permute-start | bytes 737288 | tf_op jit(solution)/shard_map/ppermute | solution.py:357
  9.2 9.4 %collective-permute-start.10 = (f32[1344,128]{1,0:T(8,128)}, f32[1344,128]{1,0:T(8,128)S(1)}, u32[]{:S(2)}, u32[]{:S(2)}) collective-permute-start(f32[1344,128]{1,0:T(8,128)} %get-tuple-element.19), channel_id=1, source_target_pairs={{0,1},{1,0},{2,3},{3,2},{4,5},{5,4},{6,7},{7,6},{8,9},{9,8},{10,11... | collective-permute-start | bytes 2064392 | tf_op jit(solution)/shard_map/ppermute | solution.py:357
  9.9 60.4 %collective-permute-start.20 = (bf16[64,1024]{1,0:T(8,128)(2,1)S(1)}, bf16[64,1024]{1,0:T(8,128)(2,1)S(1)}, u32[]{:S(2)}, u32[]{:S(2)}) collective-permute-start(bf16[64,1024]{1,0:T(8,128)(2,1)S(1)} %copy-done.4), channel_id=1, source_target_pairs={{0,4},{1,5},{2,6},{3,7},{4,0},{5,1},{6,2},{7,3},{8,12},{9,13},{10,... | collective-permute-start | bytes 393224 | tf_op jit(solution)/shard_map/ppermute | solution.py:357
  15.2 4.8 %collective-permute-start.2 = (f32[120,128]{1,0:T(8,128)S(1)}, f32[120,128]{1,0:T(8,128)S(1)}, u32[]{:S(2)}, u32[]{:S(2)}) collective-permute-start(f32[120,128]{1,0:T(8,128)S(1)} %get-tuple-element.34), channel_id=1, source_target_pairs={{0,4},{1,5},{2,6},{3,7},{4,0},{5,1},{6,2},{7,3},{8,12},{9,13},{10,... | collective-permute-start | bytes 184328 | tf_op jit(solution)/shard_map/ppermute | solution.py:357
  15.5 4.7 %collective-permute-start.3 = (f32[120,128]{1,0:T(8,128)S(1)}, f32[120,128]{1,0:T(8,128)S(1)}, u32[]{:S(2)}, u32[]{:S(2)}) collective-permute-start(f32[120,128]{1,0:T(8,128)S(1)} %get-tuple-element.36), channel_id=1, source_target_pairs={{0,8},{1,9},{2,10},{3,11},{4,12},{5,13},{6,14},{7,15},{8,0},{9,1},... | collective-permute-start | bytes 184328 | tf_op jit(solution)/shard_map/ppermute | solution.py:357
  17.8 3.1 %collective-permute-start.4 = (f32[120,128]{1,0:T(8,128)S(1)}, f32[120,128]{1,0:T(8,128)S(1)}, u32[]{:S(2)}, u32[]{:S(2)}) collective-permute-start(f32[120,128]{1,0:T(8,128)S(1)} %get-tuple-element.35), channel_id=1, source_target_pairs={{0,12},{1,13},{2,14},{3,15},{4,8},{5,9},{6,10},{7,11},{8,4},{9,5},... | collective-permute-start | bytes 184328 | tf_op jit(solution)/shard_map/ppermute | solution.py:357
  18.7 10.5 %collective-permute-start.11 = (f32[672,128]{1,0:T(8,128)S(1)}, f32[672,128]{1,0:T(8,128)S(1)}, u32[]{:S(2)}, u32[]{:S(2)}) collective-permute-start(f32[672,128]{1,0:T(8,128)S(1)} %slice.55), channel_id=1, source_target_pairs={{0,2},{1,3},{2,0},{3,1},{4,6},{5,7},{6,4},{7,5},{8,10},{9,11},{10,... | collective-permute-start | bytes 1032200 | tf_op jit(solution)/shard_map/ppermute | solution.py:357
  20.9 5.1 %collective-permute-start.5 = (f32[120,128]{1,0:T(8,128)S(1)}, f32[120,128]{1,0:T(8,128)S(1)}, u32[]{:S(2)}, u32[]{:S(2)}) collective-permute-start(f32[120,128]{1,0:T(8,128)S(1)} %get-tuple-element.30), channel_id=1, source_target_pairs={{0,4},{1,5},{2,6},{3,7},{4,0},{5,1},{6,2},{7,3},{8,12},{9,13},{10,... | collective-permute-start | bytes 184328 | tf_op jit(solution)/shard_map/ppermute | solution.py:357
  24.0 4.1 %collective-permute-start.6 = (f32[120,128]{1,0:T(8,128)S(1)}, f32[120,128]{1,0:T(8,128)S(1)}, u32[]{:S(2)}, u32[]{:S(2)}) collective-permute-start(f32[120,128]{1,0:T(8,128)S(1)} %get-tuple-element.30), channel_id=1, source_target_pairs={{0,8},{1,9},{2,10},{3,11},{4,12},{5,13},{6,14},{7,15},{8,0},{9,1},... | collective-permute-start | bytes 184328 | tf_op jit(solution)/shard_map/ppermute | solution.py:357
  24.2 4.9 %collective-permute-start.7 = (f32[120,128]{1,0:T(8,128)S(1)}, f32[120,128]{1,0:T(8,128)S(1)}, u32[]{:S(2)}, u32[]{:S(2)}) collective-permute-start(f32[120,128]{1,0:T(8,128)S(1)} %get-tuple-element.30), channel_id=1, source_target_pairs={{0,12},{1,13},{2,14},{3,15},{4,8},{5,9},{6,10},{7,11},{8,4},{9,5},... | collective-permute-start | bytes 184328 | tf_op jit(solution)/shard_map/ppermute | solution.py:357
  26.0 44.3 %collective-permute-start.21 = (bf16[64,1024]{1,0:T(8,128)(2,1)S(1)}, bf16[64,1024]{1,0:T(8,128)(2,1)S(1)}, u32[]{:S(2)}, u32[]{:S(2)}) collective-permute-start(bf16[64,1024]{1,0:T(8,128)(2,1)S(1)} %copy-done.4), channel_id=1, source_target_pairs={{0,8},{1,9},{2,10},{3,11},{4,12},{5,13},{6,14},{7,15},{8,0},{9,1},... | collective-permute-start | bytes 393224 | tf_op jit(solution)/shard_map/ppermute | solution.py:357
  29.2 40.0 %copy-start.1 = (bf16[1024,1024]{1,0:T(8,128)(2,1)S(1)}, bf16[1024,1024]{1,0:T(8,128)(2,1)}, u32[]{:S(2)}) copy-start(bf16[1024,1024]{1,0:T(8,128)(2,1)} %t_ref.3) | copy-start | bytes 6291460
  29.3 4.1 %collective-permute-start.12 = (f32[168,128]{1,0:T(8,128)S(1)}, f32[168,128]{1,0:T(8,128)S(1)}, u32[]{:S(2)}, u32[]{:S(2)}) collective-permute-start(f32[168,128]{1,0:T(8,128)S(1)} %get-tuple-element.31), channel_id=1, source_target_pairs={{0,4},{1,5},{2,6},{3,7},{4,0},{5,1},{6,2},{7,3},{8,12},{9,13},{10,... | collective-permute-start | bytes 258056 | tf_op jit(solution)/shard_map/ppermute | solution.py:357
  30.2 9.1 %collective-permute-start.13 = (f32[168,128]{1,0:T(8,128)S(1)}, f32[168,128]{1,0:T(8,128)S(1)}, u32[]{:S(2)}, u32[]{:S(2)}) collective-permute-start(f32[168,128]{1,0:T(8,128)S(1)} %get-tuple-element.33), channel_id=1, source_target_pairs={{0,8},{1,9},{2,10},{3,11},{4,12},{5,13},{6,14},{7,15},{8,0},{9,1},... | collective-permute-start | bytes 258056 | tf_op jit(solution)/shard_map/ppermute | solution.py:357
  31.8 9.6 %collective-permute-start.14 = (f32[168,128]{1,0:T(8,128)S(1)}, f32[168,128]{1,0:T(8,128)S(1)}, u32[]{:S(2)}, u32[]{:S(2)}) collective-permute-start(f32[168,128]{1,0:T(8,128)S(1)} %get-tuple-element.32), channel_id=1, source_target_pairs={{0,12},{1,13},{2,14},{3,15},{4,8},{5,9},{6,10},{7,11},{8,4},{9,5},... | collective-permute-start | bytes 258056 | tf_op jit(solution)/shard_map/ppermute | solution.py:357
  41.4 4.4 %collective-permute-start.15 = (f32[168,128]{1,0:T(8,128)S(1)}, f32[168,128]{1,0:T(8,128)S(1)}, u32[]{:S(2)}, u32[]{:S(2)}) collective-permute-start(f32[168,128]{1,0:T(8,128)S(1)} %get-tuple-element.28), channel_id=1, source_target_pairs={{0,4},{1,5},{2,6},{3,7},{4,0},{5,1},{6,2},{7,3},{8,12},{9,13},{10,... | collective-permute-start | bytes 258056 | tf_op jit(solution)/shard_map/ppermute | solution.py:357
  41.8 8.1 %collective-permute-start.16 = (f32[168,128]{1,0:T(8,128)S(1)}, f32[168,128]{1,0:T(8,128)S(1)}, u32[]{:S(2)}, u32[]{:S(2)}) collective-permute-start(f32[168,128]{1,0:T(8,128)S(1)} %get-tuple-element.28), channel_id=1, source_target_pairs={{0,8},{1,9},{2,10},{3,11},{4,12},{5,13},{6,14},{7,15},{8,0},{9,1},... | collective-permute-start | bytes 258056 | tf_op jit(solution)/shard_map/ppermute | solution.py:357
  43.8 8.1 %collective-permute-start.17 = (f32[168,128]{1,0:T(8,128)S(1)}, f32[168,128]{1,0:T(8,128)S(1)}, u32[]{:S(2)}, u32[]{:S(2)}) collective-permute-start(f32[168,128]{1,0:T(8,128)S(1)} %get-tuple-element.28), channel_id=1, source_target_pairs={{0,12},{1,13},{2,14},{3,15},{4,8},{5,9},{6,10},{7,11},{8,4},{9,5},... | collective-permute-start | bytes 258056 | tf_op jit(solution)/shard_map/ppermute | solution.py:357
  45.8 24.5 %collective-permute-start.22 = (bf16[64,1024]{1,0:T(8,128)(2,1)S(1)}, bf16[64,1024]{1,0:T(8,128)(2,1)S(1)}, u32[]{:S(2)}, u32[]{:S(2)}) collective-permute-start(bf16[64,1024]{1,0:T(8,128)(2,1)S(1)} %copy-done.4), channel_id=1, source_target_pairs={{0,12},{1,13},{2,14},{3,15},{4,8},{5,9},{6,10},{7,11},{8,4},{9,5},... | collective-permute-start | bytes 393224 | tf_op jit(solution)/shard_map/ppermute | solution.py:357
  49.9 19.2 %collective-permute-start.8 = (f32[480,128]{1,0:T(8,128)S(1)}, f32[480,128]{1,0:T(8,128)S(1)}, u32[]{:S(2)}, u32[]{:S(2)}) collective-permute-start(f32[480,128]{1,0:T(8,128)S(1)} %pad_maximum_fusion.2), channel_id=1, source_target_pairs={{0,2},{1,3},{2,0},{3,1},{4,6},{5,7},{6,4},{7,5},{8,10},{9,11},{10,... | collective-permute-start | bytes 737288 | tf_op jit(solution)/shard_map/ppermute | solution.py:357
  51.9 7.1 %collective-permute-start.18 = (f32[672,128]{1,0:T(8,128)S(1)}, f32[672,128]{1,0:T(8,128)S(1)}, u32[]{:S(2)}, u32[]{:S(2)}) collective-permute-start(f32[672,128]{1,0:T(8,128)S(1)} %pad_maximum_fusion.1), channel_id=1, source_target_pairs={{0,2},{1,3},{2,0},{3,1},{4,6},{5,7},{6,4},{7,5},{8,10},{9,11},{10,... | collective-permute-start | bytes 1032200 | tf_op jit(solution)/shard_map/ppermute | solution.py:357
  59.0 14.7 %copy-start.5 = (f32[1344,128]{1,0:T(8,128)}, f32[1344,128]{1,0:T(8,128)S(1)}, u32[]{:S(2)}) copy-start(f32[1344,128]{1,0:T(8,128)S(1)} %constant_dynamic-update-slice_fusion.5.refs_2_) | copy-start | bytes 2064388
  59.0 12.6 %collective-permute-start.19 = (f32[1344,128]{1,0:T(8,128)S(1)}, f32[1344,128]{1,0:T(8,128)S(1)}, u32[]{:S(2)}, u32[]{:S(2)}) collective-permute-start(f32[1344,128]{1,0:T(8,128)S(1)} %constant_dynamic-update-slice_fusion.5.refs_2_), channel_id=1, source_target_pairs={{0,1},{1,0},{2,3},{3,2},{4,5},{5,4},{6,7},{7,6},{8,9},{9,8},{10,11... | collective-permute-start | bytes 2064392 | tf_op jit(solution)/shard_map/ppermute | solution.py:357
  69.1 2.4 %collective-permute-start.9 = (f32[960,128]{1,0:T(8,128)S(1)}, f32[960,128]{1,0:T(8,128)S(1)}, u32[]{:S(2)}, u32[]{:S(2)}) collective-permute-start(f32[960,128]{1,0:T(8,128)S(1)} %constant_dynamic-update-slice_fusion.refs_0_), channel_id=1, source_target_pairs={{0,1},{1,0},{2,3},{3,2},{4,5},{5,4},{6,7},{7,6},{8,9},{9,8},{10,11... | collective-permute-start | bytes 1474568 | tf_op jit(solution)/shard_map/ppermute | solution.py:357
  70.3 49.3 %copy-start.3 = (bf16[256,1024]{1,0:T(8,128)(2,1)}, bf16[256,1024]{1,0:T(8,128)(2,1)S(1)}, u32[]{:S(2)}) copy-start(bf16[256,1024]{1,0:T(8,128)(2,1)S(1)} %pad_maximum_fusion.refs_0_) | copy-start | bytes 1572868
  71.6 48.1 %collective-permute-start.23 = (bf16[256,1024]{1,0:T(8,128)(2,1)S(1)}, bf16[256,1024]{1,0:T(8,128)(2,1)S(1)}, u32[]{:S(2)}, u32[]{:S(2)}) collective-permute-start(bf16[256,1024]{1,0:T(8,128)(2,1)S(1)} %pad_maximum_fusion.refs_0_), channel_id=1, source_target_pairs={{0,1},{1,0},{2,3},{3,2},{4,5},{5,4},{6,7},{7,6},{8,9},{9,8},{10,11... | collective-permute-start | bytes 1572872 | tf_op jit(solution)/shard_map/ppermute | solution.py:357
  72.0 47.7 %collective-permute-start.24 = (bf16[256,1024]{1,0:T(8,128)(2,1)S(1)}, bf16[256,1024]{1,0:T(8,128)(2,1)S(1)}, u32[]{:S(2)}, u32[]{:S(2)}) collective-permute-start(bf16[256,1024]{1,0:T(8,128)(2,1)S(1)} %pad_maximum_fusion.refs_0_), channel_id=1, source_target_pairs={{0,2},{1,3},{2,0},{3,1},{4,6},{5,7},{6,4},{7,5},{8,10},{9,11},{10,... | collective-permute-start | bytes 1572872 | tf_op jit(solution)/shard_map/ppermute | solution.py:357
  73.3 46.4 %collective-permute-start.25 = (bf16[256,1024]{1,0:T(8,128)(2,1)S(1)}, bf16[256,1024]{1,0:T(8,128)(2,1)S(1)}, u32[]{:S(2)}, u32[]{:S(2)}) collective-permute-start(bf16[256,1024]{1,0:T(8,128)(2,1)S(1)} %pad_maximum_fusion.refs_0_), channel_id=1, source_target_pairs={{0,3},{1,2},{2,1},{3,0},{4,7},{5,6},{6,5},{7,4},{8,11},{9,10},{10,... | collective-permute-start | bytes 1572872 | tf_op jit(solution)/shard_map/ppermute | solution.py:357
  (7 other events, 21.8 us)

commit v3 on v2

--- a/solution.py
+++ b/solution.py
@@ -15,7 +15,7 @@
 NT = (((1,), (1,)), ((), ()))
 NN = (((1,), (0,)), ((), ()))
 TN = (((0,), (0,)), ((), ()))
-VMEM_BYTES = 56 * 1024 * 1024
+MIB = 1024 * 1024
 
 
 def dot(a, b, dims):
@@ -70,9 +70,9 @@
             c = chunk_of(j)
             o = slab_offset(j, nb) - plan[c][2]
             packs[c][o : o + width - B * j, :] = g[B * h :, B * h : B * h + B]
-    me = me_ref[0]
     half = pieces // 2
     for c, (first, last, start, rows) in enumerate(plan):
+        me = me_ref[c]
         used = slab_offset(last, nb) - start
         if used < pieces * rows:
             packs[c][used:, :] = jnp.zeros((pieces * rows - used, B), F32)
@@ -96,7 +96,7 @@
         ],
         out_specs=[pl.BlockSpec(memory_space=pltpu.VMEM) for _ in halves],
         scratch_shapes=[pltpu.VMEM((pieces * p[3], B), F32) for p in plan],
-        compiler_params=pltpu.CompilerParams(vmem_limit_bytes=VMEM_BYTES),
+        compiler_params=pltpu.CompilerParams(vmem_limit_bytes=24 * MIB),
         cost_estimate=pl.CostEstimate(
             flops=t.shape[0] * t.shape[1] * t.shape[1],
             bytes_accessed=t.size * 2 + sum(h.size for h in halves) * 4,
@@ -179,9 +179,9 @@
     count = len(plan)
     parts, (hi_ref, lo_ref), packs = refs[: 2 * count], refs[2 * count : 2 * count + 2], refs[2 * count + 2 : 3 * count + 2]
     A, D, inv, spread, W, WL, CL, CR = refs[3 * count + 2 :]
-    me = me_ref[0]
     half = pieces // 2
     for c, (_, _, _, rows) in enumerate(plan):
+        me = me_ref[c]
         for q in range(pieces):
             to = pl.multiple_of((me ^ q) * rows, 8)
             p = q % half
@@ -287,7 +287,7 @@
             pltpu.VMEM((width, 6 * B), BF16),
             pltpu.VMEM((width, 6 * B), BF16),
         ],
-        compiler_params=pltpu.CompilerParams(vmem_limit_bytes=VMEM_BYTES),
+        compiler_params=pltpu.CompilerParams(vmem_limit_bytes=32 * MIB),
         cost_estimate=pl.CostEstimate(
             flops=12 * width**3, bytes_accessed=width * width * 8, transcendentals=0
         ),
@@ -295,16 +295,15 @@
     )(me, *parts)
 
 
-def score_kernel(me_ref, flag_ref, hi_ref, lo_ref, t_ref, scale_ref, *refs, rows):
+def score_kernel(me_ref, flag_ref, hi_ref, lo_ref, t_ref, scale_ref, *refs, rows, masks):
     parts, out_ref, evals = refs[:-2], refs[-2], refs[-1]
     e = pl.program_id(0)
 
     @pl.when(e == 0)
     def _():
-        for q2, part in enumerate(parts):
-            for q in range(part.shape[0] // rows):
-                owner = me_ref[0] ^ (q * len(parts) + q2)
-                to = pl.multiple_of(owner * rows, 16)
+        for part, held in zip(parts, masks):
+            for q, mask in enumerate(held):
+                to = pl.multiple_of((me_ref[0] ^ mask) * rows, 16)
                 evals[pl.ds(to, rows), :] = part[q * rows : (q + 1) * rows, :]
 
     @pl.when(flag_ref[e] > 0)
@@ -319,7 +318,7 @@
         out_ref[pl.ds(e, 1), :] = jnp.zeros((1, out_ref.shape[1]), F32)
 
 
-def scores(index, flags, parts, rows, hi, lo, t, scale):
+def scores(index, flags, parts, masks, rows, hi, lo, t, scale):
     total = sum(p.shape[0] for p in parts)
     blocks = total // EB
     width = t.shape[1]
@@ -327,13 +326,13 @@
     smem = pl.BlockSpec(memory_space=pltpu.SMEM)
     operands = (hi, lo, t, scale) + tuple(parts)
     return pl.pallas_call(
-        functools.partial(score_kernel, rows=rows),
+        functools.partial(score_kernel, rows=rows, masks=masks),
         grid=(blocks,),
         out_shape=jax.ShapeDtypeStruct((blocks, t.shape[0]), F32),
         in_specs=[smem, smem] + [whole(x.shape) for x in operands],
         out_specs=whole((blocks, t.shape[0])),
         scratch_shapes=[pltpu.VMEM((total, width), BF16)],
-        compiler_params=pltpu.CompilerParams(vmem_limit_bytes=VMEM_BYTES),
+        compiler_params=pltpu.CompilerParams(vmem_limit_bytes=20 * MIB + 8 * total * width),
         cost_estimate=pl.CostEstimate(
             flops=6 * total * width * width,
             bytes_accessed=total * width * 2 + width * width * 6,
@@ -357,9 +356,14 @@
     return lax.ppermute(x, "dp", [(i, i ^ mask) for i in range(n)])
 
 
-def place_of(index, n):
+def exchange_orders(n):
+    groups = bit_groups(n)
+    return [groups[:1] + groups[:0:-1], groups]
+
+
+def place_of(index, order, n):
     place, step = 0, n
-    for group in bit_groups(n):
+    for group in order:
         size = 1 << len(group)
         step //= size
         place = place + (index // group[0]) % size * step
@@ -370,37 +374,54 @@
     return [x] + [send(x, q * group[0], n) for q in range(1, 1 << len(group))]
 
 
-def all_reduce(chunks, n):
-    groups = bit_groups(n)
-    chunks = [keep + send(other, groups[0][0], n) for keep, other in chunks]
-    for group in groups[1:]:
-        size = 1 << len(group)
+def gather_stage(x, masks, group, n):
+    steps = [q * group[0] for q in range(1 << len(group))]
+    return jnp.concatenate(spread_out(x, group, n)), [m ^ step for step in steps for m in masks]
+
+
+def all_reduce(chunks, evals, orders, n):
+    first = orders[0][0][0]
+    chunks = [keep + send(other, first, n) for keep, other in chunks]
+    groups, masks = bit_groups(n), [0]
+    for group in groups[1:2] + groups[3:]:
+        evals, masks = gather_stage(evals, masks, group, n)
+    stages = len(orders[0])
+    for s in range(1, stages):
         after = []
-        for x in chunks:
+        for x, order in zip(chunks, orders):
+            size = 1 << len(order[s])
             part = x.shape[0] // size
             total = x[:part]
             for q in range(1, size):
-                total = total + send(x[q * part : (q + 1) * part], q * group[0], n)
+                total = total + send(x[q * part : (q + 1) * part], q * order[s][0], n)
             after.append(total)
-        chunks = after
-    for group in reversed(groups[1:]):
-        chunks = [jnp.concatenate(spread_out(x, group, n)) for x in chunks]
-    return [(x, send(x, groups[0][0], n)) for x in chunks]
+        chunks, evals = lax.optimization_barrier((after, evals))
+    for s in range(stages - 1, 0, -1):
+        chunks = [
+            jnp.concatenate(spread_out(x, order[s], n)) for x, order in zip(chunks, orders)
+        ]
+        chunks = lax.optimization_barrier(chunks)
+    return [(x, send(x, first, n)) for x in chunks], evals, masks
 
 
 def per_device(train_grads, eval_grads, pair_eval, pair_count, n):
     width = train_grads.shape[1]
     nb = width // B
     index = lax.axis_index("dp")
-    evals = eval_grads
-    for group in bit_groups(n)[2:]:
-        evals = jnp.concatenate(spread_out(evals, group, n))
-    me = place_of(index, n)[None]
+    orders = exchange_orders(n)
+    me = jnp.stack([place_of(index, order, n) for order in orders])
     halves = local_gram(me, train_grads, n)
-    chunks = all_reduce(list(zip(halves[::2], halves[1::2])), n)
+    chunks, evals, masks = all_reduce(
+        list(zip(halves[::2], halves[1::2])), eval_grads, orders, n
+    )
     chunks, evals = lax.optimization_barrier((chunks, evals))
-    parts = spread_out(evals, [1, 2], n)
+    groups = bit_groups(n)
+    for group in groups[2:3]:
+        evals, masks = gather_stage(evals, masks, group, n)
     hi, lo = gram_inverse(me, [x for pair in chunks for x in pair], nb, n)
+    evals, hi = lax.optimization_barrier((evals, hi))
+    parts = spread_out(evals, groups[0], n)
+    masks = [masks, [m ^ groups[0][0] for m in masks]]
     blocks = eval_grads.shape[0] * n // EB
     squares = jnp.sum(jnp.square(train_grads.astype(F32)), axis=1)
     scale = lax.rsqrt(squares + EPSILON)[None, :]
@@ -408,7 +429,7 @@
     hits = order[:, None] == jnp.arange(blocks, dtype=jnp.int32)[None, :]
     inside = jnp.arange(order.shape[0], dtype=jnp.int32)[:, None] < count
     flags = jnp.any(hits & inside, axis=0).astype(jnp.int32)
-    return scores(index[None], flags, parts, eval_grads.shape[0], hi, lo, train_grads, scale)
+    return scores(index[None], flags, parts, masks, eval_grads.shape[0], hi, lo, train_grads, scale)
 
 
 def solution(mesh):

time: 133 us -> 120 us (0.902)
  Pallas kernels: 61.9 us -> 54.3 us
  starting transfers between devices: 34.4 us -> 28.7 us
  local copies, waits for them, and re-layouts: 2.08 us -> 6.57 us
  waiting for transfers between devices: 30 us -> 27.4 us
  other arithmetic: 3.78 us -> 1.74 us
    ppermute x26 -> x25, starting transfers between devices: 34.4 us -> 28.7 us  [send(): return lax.ppermute(x, 'dp', [(i, i ^ mask) for i in range(n)])]
    unnamed x32 -> x18, local copies, waits for them, and re-layouts: 1.2 us -> 5.72 us
    pallas_call x1, Pallas kernels: 45.9 us -> 42.7 us  [gram_inverse(): pl.pallas_call(functools.partial(inverse_kernel, nb=nb, pieces=pieces), o...]
    ppermute x26 -> x25, waiting for transfers between devices: 30 us -> 27.4 us  [send(): return lax.ppermute(x, 'dp', [(i, i ^ mask) for i in range(n)])]
    pallas_call x1, Pallas kernels: 11.5 us -> 9.36 us  [scores(): pl.pallas_call(functools.partial(score_kernel, rows=rows, masks=masks), g...]
    pallas_call x1, Pallas kernels: 4.42 us -> 2.3 us  [local_gram(): pl.pallas_call(functools.partial(gram_kernel, nb=nb, pieces=pieces), out_...]
  transfers between devices with their start and end apart: 26 -> 25, of which waited for: 14 -> 15; matrix products, arithmetic and copies ran while one was open for 3% -> 2% of each run, Pallas kernels for 35% -> 36%
where the time goes in v3:
time: 120 us; the launch traced here: 119 us
  Pallas kernels  54.3 us (45%)
  starting transfers between devices  28.7 us (24%)
  waiting for transfers between devices  27.4 us (23%)
  local copies, waits for them, and re-layouts  6.57 us (5%)
  other arithmetic  1.74 us (1%)
    pallas_call x1, Pallas kernels, gram_inverse(): pl.pallas_call(functools.partial(inverse_kernel, nb=nb, pieces=pieces), o...  42.7 us
    ppermute x25, starting transfers between devices, send(): return lax.ppermute(x, 'dp', [(i, i ^ mask) for i in range(n)])  28.7 us
    ppermute x25, waiting for transfers between devices, send(): return lax.ppermute(x, 'dp', [(i, i ^ mask) for i in range(n)])  27.4 us
    pallas_call x1, Pallas kernels, scores(): pl.pallas_call(functools.partial(score_kernel, rows=rows, masks=masks), g...  9.36 us
    unnamed x18, local copies, waits for them, and re-layouts  5.72 us
  transfers between devices with their start and end apart: 25, of which 15 were waited for; matrix products, arithmetic and copies ran while one was open for 2% of the time, Pallas kernels for 36%

profile of v3, /device:TPU:11, one launch (start us, length us, event | category | flops | bytes accessed | tf_op | source)
XLA Modules:
  0.0 118.9 jit_solution(4905549573314092591)
XLA Ops:
  0.1 1.6 %copy-done.1 = bf16[1024,1024]{1,0:T(8,128)(2,1)S(1)} copy-done((bf16[1024,1024]{1,0:T(8,128)(2,1)S(1)}, bf16[1024,1024]{1,0:T(8,128)(2,1)}, u32[]{:S(2)}) %copy-start.1) | copy-done | bytes 2097176
  1.7 2.3 %local_gram.1 = (f32[960,128]{1,0:T(8,128)S(1)}, f32[960,128]{1,0:T(8,128)S(1)}, f32[1344,128]{1,0:T(8,128)S(1)}, f32[1344,128]{1,0:T(8,128)S(1)}) custom-call(s32[2]{0:T(128)S(1)} %pad_add_fusion.me_ref, bf16[1024,1024]{1,0:T(8,128)(2,1)S(1)} %copy-done.1), custom_call_target="tpu_custom_call" | custom-call | flops 1073741824 | bytes 4456448 | tf_op jit(solution)/shard_map/local_gram/pallas_call | solution.py:90
  4.0 0.7 collective-permute-start
  4.8 1.2 %collective-permute-start.6 = (bf16[64,1024]{1,0:T(8,128)(2,1)S(1)}, bf16[64,1024]{1,0:T(8,128)(2,1)S(1)}, u32[]{:S(2)}, u32[]{:S(2)}) collective-permute-start(bf16[64,1024]{1,0:T(8,128)(2,1)S(1)} %copy-done.7), channel_id=1, source_target_pairs={{0,2},{1,3},{2,0},{3,1},{4,6},{5,7},{6,4},{7,5},{8,10},{9,11},{10,... | collective-permute-start | bytes 393224 | tf_op jit(solution)/shard_map/ppermute | solution.py:356
  6.5 2.3 %collective-permute-start.2 = (f32[240,128]{1,0:T(8,128)S(1)}, f32[240,128]{1,0:T(8,128)S(1)}, u32[]{:S(2)}, u32[]{:S(2)}) collective-permute-start(f32[240,128]{1,0:T(8,128)S(1)} %get-tuple-element.53), channel_id=1, source_target_pairs={{0,8},{1,9},{2,10},{3,11},{4,12},{5,13},{6,14},{7,15},{8,0},{9,1},... | collective-permute-start | bytes 368648 | tf_op jit(solution)/shard_map/ppermute | solution.py:356
  9.1 1.3 %collective-permute-start.5 = (f32[672,128]{1,0:T(8,128)S(1)}, f32[672,128]{1,0:T(8,128)S(1)}, u32[]{:S(2)}, u32[]{:S(2)}) collective-permute-start(f32[672,128]{1,0:T(8,128)S(1)} %slice.53), channel_id=1, source_target_pairs={{0,2},{1,3},{2,0},{3,1},{4,6},{5,7},{6,4},{7,5},{8,10},{9,11},{10,... | collective-permute-start | bytes 1032200 | tf_op jit(solution)/shard_map/ppermute | solution.py:356
  10.7 3.6 %collective-permute-done.2 = f32[240,128]{1,0:T(8,128)S(1)} collective-permute-done((f32[240,128]{1,0:T(8,128)S(1)}, f32[240,128]{1,0:T(8,128)S(1)}, u32[]{:S(2)}, u32[]{:S(2)}) %collective-permute-start.2) | collective-permute-done | bytes 122912 | tf_op jit(solution)/shard_map/ppermute | solution.py:356
  14.3 5.2 %collective-permute-done.3 = f32[240,128]{1,0:T(8,128)S(1)} collective-permute-done((f32[240,128]{1,0:T(8,128)S(1)}, f32[240,128]{1,0:T(8,128)S(1)}, u32[]{:S(2)}, u32[]{:S(2)}) %collective-permute-start.3) | collective-permute-done | bytes 122912 | tf_op jit(solution)/shard_map/ppermute | solution.py:356
  19.7 1.5 %collective-permute-start.7 = (f32[120,128]{1,0:T(8,128)S(1)}, f32[120,128]{1,0:T(8,128)S(1)}, u32[]{:S(2)}, u32[]{:S(2)}) collective-permute-start(f32[120,128]{1,0:T(8,128)S(1)} %slice.43), channel_id=1, source_target_pairs={{0,2},{1,3},{2,0},{3,1},{4,6},{5,7},{6,4},{7,5},{8,10},{9,11},{10,... | collective-permute-start | bytes 184328 | tf_op jit(solution)/shard_map/ppermute | solution.py:356
  21.2 1.4 %collective-permute-start.10 = (f32[168,128]{1,0:T(8,128)S(1)}, f32[168,128]{1,0:T(8,128)S(1)}, u32[]{:S(2)}, u32[]{:S(2)}) collective-permute-start(f32[168,128]{1,0:T(8,128)S(1)} %get-tuple-element.55), channel_id=1, source_target_pairs={{0,12},{1,13},{2,14},{3,15},{4,8},{5,9},{6,10},{7,11},{8,4},{9,5},... | collective-permute-start | bytes 258056 | tf_op jit(solution)/shard_map/ppermute | solution.py:356
  22.6 0.8 collective-permute-start.8
  23.9 1.3 %collective-permute-done.10 = f32[168,128]{1,0:T(8,128)S(1)} collective-permute-done((f32[168,128]{1,0:T(8,128)S(1)}, f32[168,128]{1,0:T(8,128)S(1)}, u32[]{:S(2)}, u32[]{:S(2)}) %collective-permute-start.10) | collective-permute-done | bytes 86048 | tf_op jit(solution)/shard_map/ppermute | solution.py:356
  25.2 1.2 %collective-permute-done.8 = f32[168,128]{1,0:T(8,128)S(1)} collective-permute-done((f32[168,128]{1,0:T(8,128)S(1)}, f32[168,128]{1,0:T(8,128)S(1)}, u32[]{:S(2)}, u32[]{:S(2)}) %collective-permute-start.8) | collective-permute-done | bytes 86048 | tf_op jit(solution)/shard_map/ppermute | solution.py:356
  26.5 2.0 %collective-permute-done.9 = f32[168,128]{1,0:T(8,128)S(1)} collective-permute-done((f32[168,128]{1,0:T(8,128)S(1)}, f32[168,128]{1,0:T(8,128)S(1)}, u32[]{:S(2)}, u32[]{:S(2)}) %collective-permute-start.9) | collective-permute-done | bytes 86048 | tf_op jit(solution)/shard_map/ppermute | solution.py:356
  28.7 2.8 %collective-permute-start.12 = (f32[168,128]{1,0:T(8,128)S(1)}, f32[168,128]{1,0:T(8,128)S(1)}, u32[]{:S(2)}, u32[]{:S(2)}) collective-permute-start(f32[168,128]{1,0:T(8,128)S(1)} %add_add_fusion), channel_id=1, source_target_pairs={{0,4},{1,5},{2,6},{3,7},{4,0},{5,1},{6,2},{7,3},{8,12},{9,13},{10,... | collective-permute-start | bytes 258056 | tf_op jit(solution)/shard_map/ppermute | solution.py:356
  31.5 1.2 %collective-permute-start.14 = (f32[168,128]{1,0:T(8,128)S(1)}, f32[168,128]{1,0:T(8,128)S(1)}, u32[]{:S(2)}, u32[]{:S(2)}) collective-permute-start(f32[168,128]{1,0:T(8,128)S(1)} %add_add_fusion), channel_id=1, source_target_pairs={{0,12},{1,13},{2,14},{3,15},{4,8},{5,9},{6,10},{7,11},{8,4},{9,5},... | collective-permute-start | bytes 258056 | tf_op jit(solution)/shard_map/ppermute | solution.py:356
  33.4 2.6 %collective-permute-done.13 = f32[168,128]{1,0:T(8,128)S(1)} collective-permute-done((f32[168,128]{1,0:T(8,128)S(1)}, f32[168,128]{1,0:T(8,128)S(1)}, u32[]{:S(2)}, u32[]{:S(2)}) %collective-permute-start.13) | collective-permute-done | bytes 86048 | tf_op jit(solution)/shard_map/ppermute | solution.py:356
  36.0 0.8 collective-permute-done.14
  36.9 1.4 %collective-permute-start.18 = (f32[672,128]{1,0:T(8,128)S(1)}, f32[672,128]{1,0:T(8,128)S(1)}, u32[]{:S(2)}, u32[]{:S(2)}) collective-permute-start(f32[672,128]{1,0:T(8,128)S(1)} %pad_maximum_fusion.3), channel_id=1, source_target_pairs={{0,2},{1,3},{2,0},{3,1},{4,6},{5,7},{6,4},{7,5},{8,10},{9,11},{10,... | collective-permute-start | bytes 1032200 | tf_op jit(solution)/shard_map/ppermute | solution.py:356
  38.3 1.9 %collective-permute-start.15 = (f32[240,128]{1,0:T(8,128)S(1)}, f32[240,128]{1,0:T(8,128)S(1)}, u32[]{:S(2)}, u32[]{:S(2)}) collective-permute-start(f32[240,128]{1,0:T(8,128)S(1)} %pad_maximum_fusion.5), channel_id=1, source_target_pairs={{0,4},{1,5},{2,6},{3,7},{4,0},{5,1},{6,2},{7,3},{8,12},{9,13},{10,... | collective-permute-start | bytes 368648 | tf_op jit(solution)/shard_map/ppermute | solution.py:356
  41.4 1.9 %collective-permute-done.15 = f32[240,128]{1,0:T(8,128)S(1)} collective-permute-done((f32[240,128]{1,0:T(8,128)S(1)}, f32[240,128]{1,0:T(8,128)S(1)}, u32[]{:S(2)}, u32[]{:S(2)}) %collective-permute-start.15) | collective-permute-done | bytes 122912 | tf_op jit(solution)/shard_map/ppermute | solution.py:356
  43.3 1.7 %collective-permute-done.16 = f32[240,128]{1,0:T(8,128)S(1)} collective-permute-done((f32[240,128]{1,0:T(8,128)S(1)}, f32[240,128]{1,0:T(8,128)S(1)}, u32[]{:S(2)}, u32[]{:S(2)}) %collective-permute-start.16) | collective-permute-done | bytes 122912 | tf_op jit(solution)/shard_map/ppermute | solution.py:356
  44.9 3.0 %collective-permute-done.17 = f32[240,128]{1,0:T(8,128)S(1)} collective-permute-done((f32[240,128]{1,0:T(8,128)S(1)}, f32[240,128]{1,0:T(8,128)S(1)}, u32[]{:S(2)}, u32[]{:S(2)}) %collective-permute-start.17) | collective-permute-done | bytes 122912 | tf_op jit(solution)/shard_map/ppermute | solution.py:356
  48.1 5.7 %collective-permute-start.20 = (f32[1344,128]{1,0:T(8,128)S(1)}, f32[1344,128]{1,0:T(8,128)S(1)}, u32[]{:S(2)}, u32[]{:S(2)}) collective-permute-start(f32[1344,128]{1,0:T(8,128)S(1)} %pad_maximum_fusion.1.refs_2_), channel_id=1, source_target_pairs={{0,1},{1,0},{2,3},{3,2},{4,5},{5,4},{6,7},{7,6},{8,9},{9,8},{10,11... | collective-permute-start | bytes 2064392 | tf_op jit(solution)/shard_map/ppermute | solution.py:356
  53.9 2.4 %collective-permute-done.19.refs_1_ = f32[960,128]{1,0:T(8,128)S(1)} collective-permute-done((f32[960,128]{1,0:T(8,128)S(1)}, f32[960,128]{1,0:T(8,128)S(1)}, u32[]{:S(2)}, u32[]{:S(2)}) %collective-permute-start.19) | collective-permute-done | bytes 491552 | tf_op jit(solution)/shard_map/ppermute | solution.py:356
  56.4 2.0 %collective-permute-start.22 = (bf16[128,1024]{1,0:T(8,128)(2,1)S(1)}, bf16[128,1024]{1,0:T(8,128)(2,1)S(1)}, u32[]{:S(2)}, u32[]{:S(2)}) collective-permute-start(bf16[128,1024]{1,0:T(8,128)(2,1)S(1)} %pad_maximum_fusion.4), channel_id=1, source_target_pairs={{0,8},{1,9},{2,10},{3,11},{4,12},{5,13},{6,14},{7,15},{8,0},{9,1},... | collective-permute-start | bytes 786440 | tf_op jit(solution)/shard_map/ppermute | solution.py:356
  59.0 42.7 %gram_inverse.1 = (bf16[1024,1024]{1,0:T(8,128)(2,1)S(1)}, bf16[1024,1024]{1,0:T(8,128)(2,1)S(1)}) custom-call(s32[2]{0:T(128)S(1)} %pad_add_fusion.me_ref, f32[960,128]{1,0:T(8,128)S(1)} %pad_maximum_fusion.2.refs_0_, f32[960,128]{1,0:T(8,128)S(1)} %collective-permute-done.19.refs_1_, f32[1344,128]{1,0:T(8,128)S(1)} %pad_maximum_fusion.1.refs_2_, ...), custom_call_target="tpu_custom_call" | custom-call | flops 12884901888 | bytes 8388608 | tf_op jit(solution)/shard_map/gram_inverse/pallas_call | solution.py:273
  101.7 1.3 %copy-done.5 = bf16[1024,1024]{1,0:T(8,128)(2,1)} copy-done((bf16[1024,1024]{1,0:T(8,128)(2,1)}, bf16[1024,1024]{1,0:T(8,128)(2,1)S(1)}, u32[]{:S(2)}) %copy-start.5) | copy-done | bytes 2097176
  103.1 1.2 %copy-done.3 = bf16[1024,1024]{1,0:T(8,128)(2,1)} copy-done((bf16[1024,1024]{1,0:T(8,128)(2,1)}, bf16[1024,1024]{1,0:T(8,128)(2,1)S(1)}, u32[]{:S(2)}) %copy-start.3) | copy-done | bytes 2097176
  104.3 1.2 %collective-permute-start.24 = (bf16[512,1024]{1,0:T(8,128)(2,1)S(1)}, bf16[512,1024]{1,0:T(8,128)(2,1)}, u32[]{:S(2)}, u32[]{:S(2)}) collective-permute-start(bf16[512,1024]{1,0:T(8,128)(2,1)S(1)} %pad_maximum_fusion.refs_0_), channel_id=1, source_target_pairs={{0,1},{1,0},{2,3},{3,2},{4,5},{5,4},{6,7},{7,6},{8,9},{9,8},{10,11... | collective-permute-start | bytes 3145736 | tf_op jit(solution)/shard_map/ppermute | solution.py:356
  107.9 1.6 %copy-done.6 = bf16[1024,1024]{1,0:T(8,128)(2,1)S(1)} copy-done((bf16[1024,1024]{1,0:T(8,128)(2,1)S(1)}, bf16[1024,1024]{1,0:T(8,128)(2,1)}, u32[]{:S(2)}) %copy-start.6) | copy-done | bytes 2097176
  109.5 9.4 %scores.1 = f32[4,1024]{1,0:T(4,128)} custom-call(s32[1]{0:T(128)} %bitcast.me_ref, s32[4]{0:T(128)S(1)} %convert_element_type.6.flag_ref, bf16[1024,1024]{1,0:T(8,128)(2,1)S(1)} %copy-done.4, bf16[1024,1024]{1,0:T(8,128)(2,1)S(1)} %copy-done.6, bf16[1024,1024]{1,0:T(8,128)(2,1)S(1)} %copy-done.2, f32[1,1024]{1,0:T(1,128)S(1)} %bitcast.5, ...), custom_call_target="tpu_custom_call" | custom-call | flops 6442450944 | bytes 8388608 | tf_op jit(solution)/shard_map/scores/pallas_call | solution.py:328
  (63 shorter events, 7.2 us)
Async XLA Ops:
  0.0 106.1 %copy-start = (s32[16,4]{0,1:T(4,128)S(1)}, s32[16,4]{0,1:T(4,128)}, u32[]{:S(2)}) copy-start(s32[16,4]{0,1:T(4,128)} %param.6) | copy-start | bytes 772
  0.1 1.6 %copy-start.1 = (bf16[1024,1024]{1,0:T(8,128)(2,1)S(1)}, bf16[1024,1024]{1,0:T(8,128)(2,1)}, u32[]{:S(2)}) copy-start(bf16[1024,1024]{1,0:T(8,128)(2,1)} %t_ref.3) | copy-start | bytes 6291460
  1.7 3.1 %copy-start.7 = (bf16[64,1024]{1,0:T(8,128)(2,1)S(1)}, bf16[64,1024]{1,0:T(8,128)(2,1)}, u32[]{:S(2)}) copy-start(bf16[64,1024]{1,0:T(8,128)(2,1)} %param.5) | copy-start | bytes 393220
  4.0 2.2 %collective-permute-start = (f32[960,128]{1,0:T(8,128)S(1)}, f32[960,128]{1,0:T(8,128)S(1)}, u32[]{:S(2)}, u32[]{:S(2)}) collective-permute-start(f32[960,128]{1,0:T(8,128)S(1)} %get-tuple-element.29), channel_id=1, source_target_pairs={{0,1},{1,0},{2,3},{3,2},{4,5},{5,4},{6,7},{7,6},{8,9},{9,8},{10,11... | collective-permute-start | bytes 1474568 | tf_op jit(solution)/shard_map/ppermute | solution.py:356
  4.7 4.3 %collective-permute-start.4 = (f32[1344,128]{1,0:T(8,128)S(1)}, f32[1344,128]{1,0:T(8,128)S(1)}, u32[]{:S(2)}, u32[]{:S(2)}) collective-permute-start(f32[1344,128]{1,0:T(8,128)S(1)} %get-tuple-element.31), channel_id=1, source_target_pairs={{0,1},{1,0},{2,3},{3,2},{4,5},{5,4},{6,7},{7,6},{8,9},{9,8},{10,11... | collective-permute-start | bytes 2064392 | tf_op jit(solution)/shard_map/ppermute | solution.py:356
  4.8 5.6 %collective-permute-start.6 = (bf16[64,1024]{1,0:T(8,128)(2,1)S(1)}, bf16[64,1024]{1,0:T(8,128)(2,1)S(1)}, u32[]{:S(2)}, u32[]{:S(2)}) collective-permute-start(bf16[64,1024]{1,0:T(8,128)(2,1)S(1)} %copy-done.7), channel_id=1, source_target_pairs={{0,2},{1,3},{2,0},{3,1},{4,6},{5,7},{6,4},{7,5},{8,10},{9,11},{10,... | collective-permute-start | bytes 393224 | tf_op jit(solution)/shard_map/ppermute | solution.py:356
  6.3 4.4 %collective-permute-start.1 = (f32[240,128]{1,0:T(8,128)S(1)}, f32[240,128]{1,0:T(8,128)S(1)}, u32[]{:S(2)}, u32[]{:S(2)}) collective-permute-start(f32[240,128]{1,0:T(8,128)S(1)} %get-tuple-element.51), channel_id=1, source_target_pairs={{0,4},{1,5},{2,6},{3,7},{4,0},{5,1},{6,2},{7,3},{8,12},{9,13},{10,... | collective-permute-start | bytes 368648 | tf_op jit(solution)/shard_map/ppermute | solution.py:356
  6.5 7.8 %collective-permute-start.2 = (f32[240,128]{1,0:T(8,128)S(1)}, f32[240,128]{1,0:T(8,128)S(1)}, u32[]{:S(2)}, u32[]{:S(2)}) collective-permute-start(f32[240,128]{1,0:T(8,128)S(1)} %get-tuple-element.53), channel_id=1, source_target_pairs={{0,8},{1,9},{2,10},{3,11},{4,12},{5,13},{6,14},{7,15},{8,0},{9,1},... | collective-permute-start | bytes 368648 | tf_op jit(solution)/shard_map/ppermute | solution.py:356
  8.8 10.7 %collective-permute-start.3 = (f32[240,128]{1,0:T(8,128)S(1)}, f32[240,128]{1,0:T(8,128)S(1)}, u32[]{:S(2)}, u32[]{:S(2)}) collective-permute-start(f32[240,128]{1,0:T(8,128)S(1)} %get-tuple-element.52), channel_id=1, source_target_pairs={{0,12},{1,13},{2,14},{3,15},{4,8},{5,9},{6,10},{7,11},{8,4},{9,5},... | collective-permute-start | bytes 368648 | tf_op jit(solution)/shard_map/ppermute | solution.py:356
  9.1 10.5 %collective-permute-start.5 = (f32[672,128]{1,0:T(8,128)S(1)}, f32[672,128]{1,0:T(8,128)S(1)}, u32[]{:S(2)}, u32[]{:S(2)}) collective-permute-start(f32[672,128]{1,0:T(8,128)S(1)} %slice.53), channel_id=1, source_target_pairs={{0,2},{1,3},{2,0},{3,1},{4,6},{5,7},{6,4},{7,5},{8,10},{9,11},{10,... | collective-permute-start | bytes 1032200 | tf_op jit(solution)/shard_map/ppermute | solution.py:356
  19.7 4.2 %collective-permute-start.7 = (f32[120,128]{1,0:T(8,128)S(1)}, f32[120,128]{1,0:T(8,128)S(1)}, u32[]{:S(2)}, u32[]{:S(2)}) collective-permute-start(f32[120,128]{1,0:T(8,128)S(1)} %slice.43), channel_id=1, source_target_pairs={{0,2},{1,3},{2,0},{3,1},{4,6},{5,7},{6,4},{7,5},{8,10},{9,11},{10,... | collective-permute-start | bytes 184328 | tf_op jit(solution)/shard_map/ppermute | solution.py:356
  21.2 4.0 %collective-permute-start.10 = (f32[168,128]{1,0:T(8,128)S(1)}, f32[168,128]{1,0:T(8,128)S(1)}, u32[]{:S(2)}, u32[]{:S(2)}) collective-permute-start(f32[168,128]{1,0:T(8,128)S(1)} %get-tuple-element.55), channel_id=1, source_target_pairs={{0,12},{1,13},{2,14},{3,15},{4,8},{5,9},{6,10},{7,11},{8,4},{9,5},... | collective-permute-start | bytes 258056 | tf_op jit(solution)/shard_map/ppermute | solution.py:356
  22.6 3.9 %collective-permute-start.8 = (f32[168,128]{1,0:T(8,128)S(1)}, f32[168,128]{1,0:T(8,128)S(1)}, u32[]{:S(2)}, u32[]{:S(2)}) collective-permute-start(f32[168,128]{1,0:T(8,128)S(1)} %get-tuple-element.54), channel_id=1, source_target_pairs={{0,4},{1,5},{2,6},{3,7},{4,0},{5,1},{6,2},{7,3},{8,12},{9,13},{10,... | collective-permute-start | bytes 258056 | tf_op jit(solution)/shard_map/ppermute | solution.py:356
  23.4 5.1 %collective-permute-start.9 = (f32[168,128]{1,0:T(8,128)S(1)}, f32[168,128]{1,0:T(8,128)S(1)}, u32[]{:S(2)}, u32[]{:S(2)}) collective-permute-start(f32[168,128]{1,0:T(8,128)S(1)} %get-tuple-element.56), channel_id=1, source_target_pairs={{0,8},{1,9},{2,10},{3,11},{4,12},{5,13},{6,14},{7,15},{8,0},{9,1},... | collective-permute-start | bytes 258056 | tf_op jit(solution)/shard_map/ppermute | solution.py:356
  28.5 4.2 %collective-permute-start.11 = (f32[120,128]{1,0:T(8,128)S(1)}, f32[120,128]{1,0:T(8,128)S(1)}, u32[]{:S(2)}, u32[]{:S(2)}) collective-permute-start(f32[120,128]{1,0:T(8,128)S(1)} %slice_add_fusion.2), channel_id=1, source_target_pairs={{0,2},{1,3},{2,0},{3,1},{4,6},{5,7},{6,4},{7,5},{8,10},{9,11},{10,... | collective-permute-start | bytes 184328 | tf_op jit(solution)/shard_map/ppermute | solution.py:356
  28.7 4.7 %collective-permute-start.12 = (f32[168,128]{1,0:T(8,128)S(1)}, f32[168,128]{1,0:T(8,128)S(1)}, u32[]{:S(2)}, u32[]{:S(2)}) collective-permute-start(f32[168,128]{1,0:T(8,128)S(1)} %add_add_fusion), channel_id=1, source_target_pairs={{0,4},{1,5},{2,6},{3,7},{4,0},{5,1},{6,2},{7,3},{8,12},{9,13},{10,... | collective-permute-start | bytes 258056 | tf_op jit(solution)/shard_map/ppermute | solution.py:356
  31.5 4.5 %collective-permute-start.13 = (f32[168,128]{1,0:T(8,128)S(1)}, f32[168,128]{1,0:T(8,128)S(1)}, u32[]{:S(2)}, u32[]{:S(2)}) collective-permute-start(f32[168,128]{1,0:T(8,128)S(1)} %add_add_fusion), channel_id=1, source_target_pairs={{0,8},{1,9},{2,10},{3,11},{4,12},{5,13},{6,14},{7,15},{8,0},{9,1},... | collective-permute-start | bytes 258056 | tf_op jit(solution)/shard_map/ppermute | solution.py:356
  31.5 5.3 %collective-permute-start.14 = (f32[168,128]{1,0:T(8,128)S(1)}, f32[168,128]{1,0:T(8,128)S(1)}, u32[]{:S(2)}, u32[]{:S(2)}) collective-permute-start(f32[168,128]{1,0:T(8,128)S(1)} %add_add_fusion), channel_id=1, source_target_pairs={{0,12},{1,13},{2,14},{3,15},{4,8},{5,9},{6,10},{7,11},{8,4},{9,5},... | collective-permute-start | bytes 258056 | tf_op jit(solution)/shard_map/ppermute | solution.py:356
  36.9 11.1 %collective-permute-start.18 = (f32[672,128]{1,0:T(8,128)S(1)}, f32[672,128]{1,0:T(8,128)S(1)}, u32[]{:S(2)}, u32[]{:S(2)}) collective-permute-start(f32[672,128]{1,0:T(8,128)S(1)} %pad_maximum_fusion.3), channel_id=1, source_target_pairs={{0,2},{1,3},{2,0},{3,1},{4,6},{5,7},{6,4},{7,5},{8,10},{9,11},{10,... | collective-permute-start | bytes 1032200 | tf_op jit(solution)/shard_map/ppermute | solution.py:356
  38.3 4.9 %collective-permute-start.15 = (f32[240,128]{1,0:T(8,128)S(1)}, f32[240,128]{1,0:T(8,128)S(1)}, u32[]{:S(2)}, u32[]{:S(2)}) collective-permute-start(f32[240,128]{1,0:T(8,128)S(1)} %pad_maximum_fusion.5), channel_id=1, source_target_pairs={{0,4},{1,5},{2,6},{3,7},{4,0},{5,1},{6,2},{7,3},{8,12},{9,13},{10,... | collective-permute-start | bytes 368648 | tf_op jit(solution)/shard_map/ppermute | solution.py:356
  40.2 4.7 %collective-permute-start.16 = (f32[240,128]{1,0:T(8,128)S(1)}, f32[240,128]{1,0:T(8,128)S(1)}, u32[]{:S(2)}, u32[]{:S(2)}) collective-permute-start(f32[240,128]{1,0:T(8,128)S(1)} %pad_maximum_fusion.5), channel_id=1, source_target_pairs={{0,8},{1,9},{2,10},{3,11},{4,12},{5,13},{6,14},{7,15},{8,0},{9,1},... | collective-permute-start | bytes 368648 | tf_op jit(solution)/shard_map/ppermute | solution.py:356
  40.7 7.3 %collective-permute-start.17 = (f32[240,128]{1,0:T(8,128)S(1)}, f32[240,128]{1,0:T(8,128)S(1)}, u32[]{:S(2)}, u32[]{:S(2)}) collective-permute-start(f32[240,128]{1,0:T(8,128)S(1)} %pad_maximum_fusion.5), channel_id=1, source_target_pairs={{0,12},{1,13},{2,14},{3,15},{4,8},{5,9},{6,10},{7,11},{8,4},{9,5},... | collective-permute-start | bytes 368648 | tf_op jit(solution)/shard_map/ppermute | solution.py:356
  48.1 8.2 %collective-permute-start.20 = (f32[1344,128]{1,0:T(8,128)S(1)}, f32[1344,128]{1,0:T(8,128)S(1)}, u32[]{:S(2)}, u32[]{:S(2)}) collective-permute-start(f32[1344,128]{1,0:T(8,128)S(1)} %pad_maximum_fusion.1.refs_2_), channel_id=1, source_target_pairs={{0,1},{1,0},{2,3},{3,2},{4,5},{5,4},{6,7},{7,6},{8,9},{9,8},{10,11... | collective-permute-start | bytes 2064392 | tf_op jit(solution)/shard_map/ppermute | solution.py:356
  53.8 2.5 %collective-permute-start.19 = (f32[960,128]{1,0:T(8,128)S(1)}, f32[960,128]{1,0:T(8,128)S(1)}, u32[]{:S(2)}, u32[]{:S(2)}) collective-permute-start(f32[960,128]{1,0:T(8,128)S(1)} %pad_maximum_fusion.2.refs_0_), channel_id=1, source_target_pairs={{0,1},{1,0},{2,3},{3,2},{4,5},{5,4},{6,7},{7,6},{8,9},{9,8},{10,11... | collective-permute-start | bytes 1474568 | tf_op jit(solution)/shard_map/ppermute | solution.py:356
  56.3 46.7 %collective-permute-start.21 = (bf16[128,1024]{1,0:T(8,128)(2,1)S(1)}, bf16[128,1024]{1,0:T(8,128)(2,1)S(1)}, u32[]{:S(2)}, u32[]{:S(2)}) collective-permute-start(bf16[128,1024]{1,0:T(8,128)(2,1)S(1)} %pad_maximum_fusion.4), channel_id=1, source_target_pairs={{0,4},{1,5},{2,6},{3,7},{4,0},{5,1},{6,2},{7,3},{8,12},{9,13},{10,... | collective-permute-start | bytes 786440 | tf_op jit(solution)/shard_map/ppermute | solution.py:356
  56.4 46.6 %collective-permute-start.22 = (bf16[128,1024]{1,0:T(8,128)(2,1)S(1)}, bf16[128,1024]{1,0:T(8,128)(2,1)S(1)}, u32[]{:S(2)}, u32[]{:S(2)}) collective-permute-start(bf16[128,1024]{1,0:T(8,128)(2,1)S(1)} %pad_maximum_fusion.4), channel_id=1, source_target_pairs={{0,8},{1,9},{2,10},{3,11},{4,12},{5,13},{6,14},{7,15},{8,0},{9,1},... | collective-permute-start | bytes 786440 | tf_op jit(solution)/shard_map/ppermute | solution.py:356
  58.4 44.6 %collective-permute-start.23 = (bf16[128,1024]{1,0:T(8,128)(2,1)S(1)}, bf16[128,1024]{1,0:T(8,128)(2,1)S(1)}, u32[]{:S(2)}, u32[]{:S(2)}) collective-permute-start(bf16[128,1024]{1,0:T(8,128)(2,1)S(1)} %pad_maximum_fusion.4), channel_id=1, source_target_pairs={{0,12},{1,13},{2,14},{3,15},{4,8},{5,9},{6,10},{7,11},{8,4},{9,5},... | collective-permute-start | bytes 786440 | tf_op jit(solution)/shard_map/ppermute | solution.py:356
  103.0 2.5 %copy-start.8 = (s32[16]{0:T(128)S(1)}, s32[16]{0:T(128)}, u32[]{:S(2)}) copy-start(s32[16]{0:T(128)} %param.7) | copy-start | bytes 196
  103.0 4.0 %copy-start.2 = (bf16[1024,1024]{1,0:T(8,128)(2,1)S(1)}, bf16[1024,1024]{1,0:T(8,128)(2,1)}, u32[]{:S(2)}) copy-start(bf16[1024,1024]{1,0:T(8,128)(2,1)} %t_ref.3) | copy-start | bytes 6291460
  104.3 3.6 %collective-permute-start.24 = (bf16[512,1024]{1,0:T(8,128)(2,1)S(1)}, bf16[512,1024]{1,0:T(8,128)(2,1)}, u32[]{:S(2)}, u32[]{:S(2)}) collective-permute-start(bf16[512,1024]{1,0:T(8,128)(2,1)S(1)} %pad_maximum_fusion.refs_0_), channel_id=1, source_target_pairs={{0,1},{1,0},{2,3},{3,2},{4,5},{5,4},{6,7},{7,6},{8,9},{9,8},{10,11... | collective-permute-start | bytes 3145736 | tf_op jit(solution)/shard_map/ppermute | solution.py:356
  105.5 2.4 %copy-start.4 = (bf16[1024,1024]{1,0:T(8,128)(2,1)S(1)}, bf16[1024,1024]{1,0:T(8,128)(2,1)}, u32[]{:S(2)}) copy-start(bf16[1024,1024]{1,0:T(8,128)(2,1)} %copy-done.3) | copy-start | bytes 6291460
  107.9 1.6 %copy-start.6 = (bf16[1024,1024]{1,0:T(8,128)(2,1)S(1)}, bf16[1024,1024]{1,0:T(8,128)(2,1)}, u32[]{:S(2)}) copy-start(bf16[1024,1024]{1,0:T(8,128)(2,1)} %copy-done.5) | copy-start | bytes 6291460
  (2 other events, 2.6 us)
